TPU v7x, 32 devices: a whole 2x2x4 slice. The times are simulated.
32 devices in a mesh: ctx: 8 (over y, x, core), fsdp: 4 (over z).
Axes of the slice: x: 2, y: 2, z: 4, core: 2. Of those that a mesh axis runs over, the one named last changes fastest.
Arguments:
- tokens: bfloat16 [4, 1024, 1024], P('fsdp', 'ctx'), may hold values from -6 to 6
- cotangent: float32 [4, 1024, 1024], P('fsdp', 'ctx'), may hold values from -6 to 6
- block_order: int32 [4, 16], P('fsdp'), may hold values from 0 to 15, each once within a row
- ln1_gain: bfloat16 [1, 1024], P(None, 'fsdp'), may hold values from 0.099609375 to 1.8984375
- ln1_bias: bfloat16 [1, 1024], P(None, 'fsdp'), may hold values from -4 to 4
- qkv_weight: bfloat16 [1, 1024, 3072], P(None, 'fsdp'), may hold values from -0.1875 to 0.1875
- query_bias: bfloat16 [1, 1024], P(None, 'fsdp'), may hold values from -6 to 6
- value_bias: bfloat16 [1, 1024], P(None, 'fsdp'), may hold values from -6 to 6
- proj_weight: bfloat16 [1, 1024, 1024], P(None, 'fsdp'), may hold values from -0.75 to 0.75
- proj_bias: bfloat16 [1, 1024], P(None, 'fsdp'), may hold values from -4 to 4
- ln2_gain: bfloat16 [1, 1024], P(None, 'fsdp'), may hold values from 0.099609375 to 1.8984375
- ln2_bias: bfloat16 [1, 1024], P(None, 'fsdp'), may hold values from -4 to 4
- fc_weight: bfloat16 [1, 1024, 4096], P(None, 'fsdp'), may hold values from -0.1875 to 0.1875
- fc_bias: bfloat16 [1, 4096], P(None, 'fsdp'), may hold values from -6 to 6
- out_weight: bfloat16 [1, 4096, 1024], P(None, 'fsdp'), may hold values from -0.09375 to 0.09375
- out_bias: bfloat16 [1, 1024], P(None, 'fsdp'), may hold values from -4 to 4
Outputs:
- block_out: float32 [4, 1024, 1024], P('fsdp', 'ctx')
- input_grad: float32 [4, 1024, 1024], P('fsdp', 'ctx')
- ln1_gain_grad: float32 [1, 1024], P(None, 'fsdp')
- ln1_bias_grad: float32 [1, 1024], P(None, 'fsdp')
- qkv_weight_grad: float32 [1, 1024, 3072], P(None, 'fsdp')
- query_bias_grad: float32 [1, 1024], P(None, 'fsdp')
- value_bias_grad: float32 [1, 1024], P(None, 'fsdp')
- proj_weight_grad: float32 [1, 1024, 1024], P(None, 'fsdp')
- proj_bias_grad: float32 [1, 1024], P(None, 'fsdp')
- ln2_gain_grad: float32 [1, 1024], P(None, 'fsdp')
- ln2_bias_grad: float32 [1, 1024], P(None, 'fsdp')
- fc_weight_grad: float32 [1, 1024, 4096], P(None, 'fsdp')
- fc_bias_grad: float32 [1, 4096], P(None, 'fsdp')
- out_weight_grad: float32 [1, 4096, 1024], P(None, 'fsdp')
- out_bias_grad: float32 [1, 1024], P(None, 'fsdp')
Inputs may be any that keep to these rules, and one draw needn't show every extreme that they name: `block_order`: each row names every number from 0 to 15 once.
All inputs are finite; a program needn't handle non-finite values.
Results may differ from a plain program's by a relative error of at most 0.014.
Values may be sent and summed in bfloat16 or wider, within the bound.
A program may use at most 192 MiB of HBM per device.

v0:
```python
from functools import partial
import math

import jax
import jax.numpy as jnp
from jax import lax
from jax.sharding import PartitionSpec as P

D = 1024
HEADS = 16
HEAD_DIM = 64
LAYERS = 1


NORM_EPS = 1e-05
GELU_SCALE = math.sqrt(2.0 / math.pi)


def layer_norm(values_in, gain_vec, shift_vec):
    center = values_in - jnp.mean(values_in, axis=-1, keepdims=True)
    variance = jnp.mean(center * center, axis=-1, keepdims=True)
    inverse = lax.rsqrt(variance + NORM_EPS)
    normed = center * inverse
    return (normed * gain_vec + shift_vec, normed, inverse)


def norm_back(upstream, normed, inverse, gain_vec):
    scaled = upstream * gain_vec
    inner_term = (
        scaled
        - jnp.mean(scaled, axis=-1, keepdims=True)
        - normed * jnp.mean(scaled * normed, axis=-1, keepdims=True)
    )
    return (inverse * inner_term, jnp.sum(upstream * normed, axis=0), jnp.sum(upstream, axis=0))


def gelu_pair(pre_act):
    inner_arg = GELU_SCALE * (pre_act + 0.044715 * pre_act * pre_act * pre_act)
    tangent = jnp.tanh(inner_arg)
    output = 0.5 * pre_act * (1.0 + tangent)
    gelu_slope = 0.5 * (1.0 + tangent) + 0.5 * pre_act * (1.0 - tangent * tangent) * GELU_SCALE * (
        1.0 + 3.0 * 0.044715 * pre_act * pre_act
    )
    return (output, gelu_slope)


def token_positions(order_row, first_row, row_total, half_block):
    index_row = first_row + jnp.arange(row_total, dtype=jnp.int32)
    slot_row = index_row // half_block
    onehot = slot_row[:, None] == jnp.arange(order_row.shape[0], dtype=jnp.int32)[None, :]
    base_row = jnp.sum(jnp.where(onehot, order_row[None, :], 0), axis=1)
    return base_row * half_block + index_row % half_block


def attend_forward(order_row, query_pos, half_block, queries, key_rows, value_rows):
    row_count = queries.shape[0]
    query_heads = queries.reshape(row_count, HEADS, HEAD_DIM)
    initial = (
        jnp.full((HEADS, row_count), -1e30, jnp.float32),
        jnp.zeros((HEADS, row_count), jnp.float32),
        jnp.zeros((row_count, HEADS, HEAD_DIM), jnp.float32),
    )
    key_piece = lax.all_gather(key_rows, "ctx", axis=0, tiled=True)
    value_piece = lax.all_gather(value_rows, "ctx", axis=0, tiled=True)
    piece_rows = key_piece.shape[0]
    key_pos = token_positions(order_row, jnp.int32(0), piece_rows, half_block)
    block_width = math.gcd(piece_rows, 512)
    block_count = piece_rows // block_width
    inputs_all = (
        key_piece.reshape(block_count, block_width, HEADS, HEAD_DIM),
        value_piece.reshape(block_count, block_width, HEADS, HEAD_DIM),
        key_pos.reshape(block_count, block_width),
    )

    def fold_one_block(run_state, inputs):
        run_max, run_sum, run_acc = run_state
        key_blk, value_blk, pos_blk = inputs
        scores = (
            jnp.einsum("qhd,khd->hqk", query_heads, key_blk, preferred_element_type=jnp.float32)
            * 0.125
        )
        allowed = pos_blk[None, None, :] <= query_pos[None, :, None]
        new_max = jnp.maximum(run_max, jnp.max(jnp.where(allowed, scores, -1e30), axis=2))
        attn_probs = jnp.where(allowed, jnp.exp(scores - new_max[:, :, None]), 0.0)
        factor = jnp.exp(run_max - new_max)
        run_sum = run_sum * factor + jnp.sum(attn_probs, axis=2)
        update = jnp.einsum(
            "hqk,khd->qhd",
            attn_probs.astype(jnp.bfloat16),
            value_blk,
            preferred_element_type=jnp.float32,
        )
        run_acc = run_acc * factor.T[:, :, None] + update
        return ((new_max, run_sum, run_acc), None)

    run_state, _ = lax.scan(fold_one_block, initial, inputs_all)
    run_max, run_sum, run_acc = run_state
    att_out = (run_acc / run_sum.T[:, :, None]).reshape(row_count, D).astype(jnp.bfloat16)
    return (att_out, run_max + jnp.log(run_sum))


def back_keys(
    order_row, query_pos, half_block, queries, key_rows, value_rows, att_out, grad_att, lse_rows
):
    row_count = queries.shape[0]
    query_heads = queries.reshape(row_count, HEADS, HEAD_DIM)
    grad_heads = grad_att.reshape(row_count, HEADS, HEAD_DIM)
    delta_rows = jnp.sum(
        grad_heads.astype(jnp.float32)
        * att_out.reshape(row_count, HEADS, HEAD_DIM).astype(jnp.float32),
        axis=2,
    ).T
    all_keys, all_values = (
        lax.all_gather(key_rows, "ctx", axis=0, tiled=True),
        lax.all_gather(value_rows, "ctx", axis=0, tiled=True),
    )
    total_rows = all_keys.shape[0]
    block_width = math.gcd(total_rows, 512)
    block_count = total_rows // block_width
    key_pos = token_positions(order_row, 0, total_rows, half_block)
    inputs_all = (
        all_keys.reshape(block_count, block_width, HEADS, HEAD_DIM),
        all_values.reshape(block_count, block_width, HEADS, HEAD_DIM),
        key_pos.reshape(block_count, block_width),
    )

    def back_one_block(grad_query, inputs):
        key_blk, value_blk, pos_blk = inputs
        scores = (
            jnp.einsum("qhd,khd->hqk", query_heads, key_blk, preferred_element_type=jnp.float32)
            * 0.125
        )
        allowed = pos_blk[None, None, :] <= query_pos[None, :, None]
        attn_probs = jnp.where(allowed, jnp.exp(scores - lse_rows[:, :, None]), 0.0)
        value_term = jnp.einsum(
            "hqk,qhd->khd",
            attn_probs.astype(jnp.bfloat16),
            grad_heads,
            preferred_element_type=jnp.float32,
        )
        grad_probs = jnp.einsum(
            "qhd,khd->hqk", grad_heads, value_blk, preferred_element_type=jnp.float32
        )
        grad_scores = (attn_probs * (grad_probs - delta_rows[:, :, None]) * 0.125).astype(
            jnp.bfloat16
        )
        grad_query = grad_query + jnp.einsum(
            "hqk,khd->qhd", grad_scores, key_blk, preferred_element_type=jnp.float32
        )
        key_term = jnp.einsum(
            "hqk,qhd->khd", grad_scores, query_heads, preferred_element_type=jnp.float32
        )
        return (grad_query, (key_term, value_term))

    zero_state = jnp.zeros((row_count, HEADS, HEAD_DIM), jnp.float32)
    grad_query, (key_terms, value_terms) = lax.scan(back_one_block, zero_state, inputs_all)
    own_keys, own_values = (
        lax.psum_scatter(key_terms.reshape(total_rows, D), "ctx", scatter_dimension=0, tiled=True),
        lax.psum_scatter(
            value_terms.reshape(total_rows, D), "ctx", scatter_dimension=0, tiled=True
        ),
    )
    return (grad_query.reshape(row_count, D), own_keys, own_values)


def layer_forward(stream, weights_now, attend_fn):
    (
        gain_one,
        shift_one,
        qkv_w,
        query_b,
        value_b,
        proj_w,
        proj_b,
        gain_two,
        shift_two,
        fc_w,
        fc_b,
        out_w,
        out_b,
    ) = weights_now
    normed_out, normed_one, inverse_one = layer_norm(
        stream, gain_one.astype(jnp.float32), shift_one.astype(jnp.float32)
    )
    attn_in = normed_out.astype(jnp.bfloat16)
    projected = jnp.dot(attn_in, qkv_w, preferred_element_type=jnp.float32)
    queries = (projected[:, :D] + query_b.astype(jnp.float32)).astype(jnp.bfloat16)
    key_rows = projected[:, D : 2 * D].astype(jnp.bfloat16)
    value_rows = (projected[:, 2 * D :] + value_b.astype(jnp.float32)).astype(jnp.bfloat16)
    att_out, lse_rows = attend_fn(queries, key_rows, value_rows)
    middle = (
        stream
        + jnp.dot(att_out, proj_w, preferred_element_type=jnp.float32)
        + proj_b.astype(jnp.float32)
    )
    normed_mid, normed_two, inverse_two = layer_norm(
        middle, gain_two.astype(jnp.float32), shift_two.astype(jnp.float32)
    )
    mlp_in = normed_mid.astype(jnp.bfloat16)
    pre_act = jnp.dot(mlp_in, fc_w, preferred_element_type=jnp.float32) + fc_b.astype(jnp.float32)
    activated, gelu_slope = gelu_pair(pre_act)
    act_rows = activated.astype(jnp.bfloat16)
    result = (
        middle
        + jnp.dot(act_rows, out_w, preferred_element_type=jnp.float32)
        + out_b.astype(jnp.float32)
    )
    record = (
        normed_one,
        inverse_one,
        attn_in,
        queries,
        key_rows,
        value_rows,
        att_out,
        lse_rows,
        normed_two,
        inverse_two,
        mlp_in,
        gelu_slope,
        act_rows,
    )
    return (result, record)


def layer_backward(upstream, weights_now, record, back_fn):
    (
        gain_one,
        shift_one,
        qkv_w,
        query_b,
        value_b,
        proj_w,
        proj_b,
        gain_two,
        shift_two,
        fc_w,
        fc_b,
        out_w,
        out_b,
    ) = weights_now
    (
        normed_one,
        inverse_one,
        attn_in,
        queries,
        key_rows,
        value_rows,
        att_out,
        lse_rows,
        normed_two,
        inverse_two,
        mlp_in,
        gelu_slope,
        act_rows,
    ) = record
    up_rows = upstream.astype(jnp.bfloat16)
    grad_out_b = jnp.sum(upstream, axis=0)
    grad_act = jnp.dot(up_rows, out_w.T, preferred_element_type=jnp.float32)
    grad_pre = grad_act * gelu_slope
    grad_pre_rows = grad_pre.astype(jnp.bfloat16)
    grad_fc_b = jnp.sum(grad_pre, axis=0)
    grad_mlp_in = jnp.dot(grad_pre_rows, fc_w.T, preferred_element_type=jnp.float32)
    back_two, grad_gain_two, grad_shift_two = norm_back(
        grad_mlp_in, normed_two, inverse_two, gain_two.astype(jnp.float32)
    )
    mid_grad = upstream + back_two
    mid_rows = mid_grad.astype(jnp.bfloat16)
    grad_proj_b = jnp.sum(mid_grad, axis=0)
    grad_att = jnp.dot(mid_rows, proj_w.T, preferred_element_type=jnp.float32).astype(jnp.bfloat16)
    grad_query, grad_key, grad_value = back_fn(
        queries, key_rows, value_rows, att_out, grad_att, lse_rows
    )
    grad_query_b = jnp.sum(grad_query, axis=0)
    grad_value_b = jnp.sum(grad_value, axis=0)
    grad_qkv_rows = jnp.concatenate([grad_query, grad_key, grad_value], axis=1).astype(jnp.bfloat16)
    grad_attn_in = jnp.dot(grad_qkv_rows, qkv_w.T, preferred_element_type=jnp.float32)
    back_one, grad_gain_one, grad_shift_one = norm_back(
        grad_attn_in, normed_one, inverse_one, gain_one.astype(jnp.float32)
    )
    new_upstream = mid_grad + back_one
    vectors = (
        grad_gain_one,
        grad_shift_one,
        grad_query_b,
        grad_value_b,
        grad_proj_b,
        grad_gain_two,
        grad_shift_two,
        grad_fc_b,
        grad_out_b,
    )
    row_pairs = (
        (attn_in, grad_qkv_rows),
        (att_out, mid_rows),
        (mlp_in, grad_pre_rows),
        (act_rows, up_rows),
    )
    return (new_upstream, vectors, row_pairs)


def assemble(vectors, matrices):
    return (
        vectors[0],
        vectors[1],
        matrices[0],
        vectors[2],
        vectors[3],
        matrices[1],
        vectors[4],
        vectors[5],
        vectors[6],
        matrices[2],
        vectors[7],
        matrices[3],
        vectors[8],
    )


def shards(
    tokens,
    cotangent,
    block_order,
    ln1_gain,
    ln1_bias,
    qkv_weight,
    query_bias,
    value_bias,
    proj_weight,
    proj_bias,
    ln2_gain,
    ln2_bias,
    fc_weight,
    fc_bias,
    out_weight,
    out_bias,
):
    row_count = tokens.shape[1]
    half_block = row_count // 2
    order_row = block_order[0]
    my_start = lax.axis_index("ctx") * row_count
    query_pos = token_positions(order_row, my_start, row_count, half_block)
    attend_fn = partial(attend_forward, order_row, query_pos, half_block)
    back_fn = partial(back_keys, order_row, query_pos, half_block)
    stream = tokens[0].astype(jnp.float32)
    layer_idx = 0
    full_weights = (
        lax.all_gather(ln1_gain[layer_idx], "fsdp", axis=0, tiled=True),
        lax.all_gather(ln1_bias[layer_idx], "fsdp", axis=0, tiled=True),
        lax.all_gather(qkv_weight[layer_idx], "fsdp", axis=0, tiled=True),
        lax.all_gather(query_bias[layer_idx], "fsdp", axis=0, tiled=True),
        lax.all_gather(value_bias[layer_idx], "fsdp", axis=0, tiled=True),
        lax.all_gather(proj_weight[layer_idx], "fsdp", axis=0, tiled=True),
        lax.all_gather(proj_bias[layer_idx], "fsdp", axis=0, tiled=True),
        lax.all_gather(ln2_gain[layer_idx], "fsdp", axis=0, tiled=True),
        lax.all_gather(ln2_bias[layer_idx], "fsdp", axis=0, tiled=True),
        lax.all_gather(fc_weight[layer_idx], "fsdp", axis=0, tiled=True),
        lax.all_gather(fc_bias[layer_idx], "fsdp", axis=0, tiled=True),
        lax.all_gather(out_weight[layer_idx], "fsdp", axis=0, tiled=True),
        lax.all_gather(out_bias[layer_idx], "fsdp", axis=0, tiled=True),
    )
    kept_weights = [full_weights]
    stream, record = layer_forward(stream, full_weights, attend_fn)
    saved_records = [record]
    upstream = cotangent[0]
    results = [None] * LAYERS
    for layer_idx in reversed(range(LAYERS)):
        full_weights = kept_weights[layer_idx]
        upstream, vectors, row_pairs = layer_backward(
            upstream, full_weights, saved_records[layer_idx], back_fn
        )
        left_slices = (
            lax.all_to_all(row_pairs[0][0], "fsdp", split_axis=1, concat_axis=0, tiled=True),
            lax.all_to_all(row_pairs[1][0], "fsdp", split_axis=1, concat_axis=0, tiled=True),
            lax.all_to_all(row_pairs[2][0], "fsdp", split_axis=1, concat_axis=0, tiled=True),
            lax.all_to_all(row_pairs[3][0], "fsdp", split_axis=1, concat_axis=0, tiled=True),
        )
        right_rows = (
            lax.all_gather(row_pairs[0][1], "fsdp", axis=0, tiled=True),
            lax.all_gather(row_pairs[1][1], "fsdp", axis=0, tiled=True),
            lax.all_gather(row_pairs[2][1], "fsdp", axis=0, tiled=True),
            lax.all_gather(row_pairs[3][1], "fsdp", axis=0, tiled=True),
        )
        matrices = tuple(
            (
                jnp.dot(
                    left_slices[pair_idx].T,
                    right_rows[pair_idx],
                    preferred_element_type=jnp.float32,
                )
                for pair_idx in range(4)
            )
        )
        vector_parts = (
            lax.psum_scatter(vectors[0], "fsdp", scatter_dimension=0, tiled=True),
            lax.psum_scatter(vectors[1], "fsdp", scatter_dimension=0, tiled=True),
            lax.psum_scatter(vectors[2], "fsdp", scatter_dimension=0, tiled=True),
            lax.psum_scatter(vectors[3], "fsdp", scatter_dimension=0, tiled=True),
            lax.psum_scatter(vectors[4], "fsdp", scatter_dimension=0, tiled=True),
            lax.psum_scatter(vectors[5], "fsdp", scatter_dimension=0, tiled=True),
            lax.psum_scatter(vectors[6], "fsdp", scatter_dimension=0, tiled=True),
            lax.psum_scatter(vectors[7], "fsdp", scatter_dimension=0, tiled=True),
            lax.psum_scatter(vectors[8], "fsdp", scatter_dimension=0, tiled=True),
        )
        shard_grads = assemble(vector_parts, matrices)
        results[layer_idx] = lax.psum(
            (
                shard_grads[0],
                shard_grads[1],
                shard_grads[2],
                shard_grads[3],
                shard_grads[4],
                shard_grads[5],
                shard_grads[6],
                shard_grads[7],
                shard_grads[8],
                shard_grads[9],
                shard_grads[10],
                shard_grads[11],
                shard_grads[12],
            ),
            "ctx",
        )
    stacked = tuple((jnp.stack([results[0][param_idx]]) for param_idx in range(13)))
    return (
        stream[None],
        upstream[None],
        stacked[0],
        stacked[1],
        stacked[2],
        stacked[3],
        stacked[4],
        stacked[5],
        stacked[6],
        stacked[7],
        stacked[8],
        stacked[9],
        stacked[10],
        stacked[11],
        stacked[12],
    )


def solution(mesh):
    placed = (
        P("fsdp", "ctx", None),
        P("fsdp", "ctx", None),
        P("fsdp", None),
        P(None, "fsdp"),
        P(None, "fsdp"),
        P(None, "fsdp", None),
        P(None, "fsdp"),
        P(None, "fsdp"),
        P(None, "fsdp", None),
        P(None, "fsdp"),
        P(None, "fsdp"),
        P(None, "fsdp"),
        P(None, "fsdp", None),
        P(None, "fsdp"),
        P(None, "fsdp", None),
        P(None, "fsdp"),
    )
    return jax.shard_map(
        shards,
        mesh=mesh,
        in_specs=placed,
        out_specs=(
            P("fsdp", "ctx", None),
            P("fsdp", "ctx", None),
            P(None, "fsdp"),
            P(None, "fsdp"),
            P(None, "fsdp", None),
            P(None, "fsdp"),
            P(None, "fsdp"),
            P(None, "fsdp", None),
            P(None, "fsdp"),
            P(None, "fsdp"),
            P(None, "fsdp"),
            P(None, "fsdp", None),
            P(None, "fsdp"),
            P(None, "fsdp", None),
            P(None, "fsdp"),
        ),
        check_vma=False,
    )
```

profile of v0, /device:TPU:0, one launch (start us, length us, event | category | flops | bytes accessed | tf_op | source)
XLA Modules:
  0.0 1269.9 jit_solution(13147615631357205537)
XLA Ops:
  8.0 12.8 %all-gather.1 = bf16[1,1024]{1,0:T(2,128)(2,1)S(1)} all-gather(bf16[1,256]{1,0:T(2,128)(2,1)} %param.24), channel_id=3, replica_groups=mesh['ctx'=8,'fsdp'=4] {'fsdp'}, dimensions={1}, use_global_device_ids=true | all-gather | bytes 2560 | tf_op jit(solution)/shard_map/all_gather | solution.py:349
  20.8 7.9 all-gather
  31.0 96.7 %all-gather.36.cloned.1.call-done = bf16[1,1024,3072]{2,1,0:T(8,128)(2,1)} async-done(((bf16[1,256,3072]{2,1,0:T(8,128)(2,1)}), bf16[1,1024,3072]{2,1,0:T(8,128)(2,1)}) %all-gather.36.cloned.1.call-update) | async-done | bytes 6291472 | tf_op jit(solution)/shard_map/all_gather | solution.py:350
  132.5 7.9 all-gather.4
  140.4 9.3 all-gather.3
  152.5 7.9 all-gather.6
  160.5 13.1 %all-gather.10 = bf16[1,4096]{1,0:T(2,128)(2,1)S(1)} all-gather(bf16[1,1024]{1,0:T(2,128)(2,1)S(1)} %copy-done.28), channel_id=12, replica_groups=mesh['ctx'=8,'fsdp'=4] {'fsdp'}, dimensions={1}, use_global_device_ids=true | all-gather | bytes 10240 | tf_op jit(solution)/shard_map/all_gather | solution.py:358
  173.6 9.3 all-gather.8
  182.9 7.9 all-gather.7
  191.2 6.4 reshape.298
  203.1 6.4 reshape.299
  214.9 20.6 %while.30 = (s32[]{:T(128)}, f32[16,128]{1,0:T(8,128)S(1)}, f32[16,128]{1,0:T(8,128)S(1)}, f32[128,16,64]{0,2,1:T(8,128)S(1)}, s32[2,512]{1,0:T(2,128)S(1)}, /*i...) while((s32[]{:T(128)}, f32[16,128]{1,0:T(8,128)S(1)}, ...), condition=%wide.region_7.8_spmd.clone, body=%wide.region_4.7_spmd.clone.sunk | while | flops 280440832 | bytes 33168040 | solution.py:96
  239.1 147.2 %all-gather.40.cloned.1.call-done = bf16[1,1024,4096]{2,1,0:T(8,128)(2,1)} async-done(((bf16[1,256,4096]{2,1,0:T(8,128)(2,1)}), bf16[1,1024,4096]{2,1,0:T(8,128)(2,1)}) %all-gather.40.cloned.1.call-update) | async-done | bytes 8388624 | tf_op jit(solution)/shard_map/all_gather | solution.py:357
  386.3 6.9 multiply_convert_fusion
  393.3 142.4 %all-gather.42.cloned.1.call-done = bf16[1,4096,1024]{2,1,0:T(8,128)(2,1)} async-done(((bf16[1,1024,1024]{2,1,0:T(8,128)(2,1)}), bf16[1,4096,1024]{2,1,0:T(8,128)(2,1)}) %all-gather.42.cloned.1.call-update) | async-done | bytes 8388624 | tf_op jit(solution)/shard_map/all_gather | solution.py:359
  535.7 7.5 fusion.116
  544.2 6.5 multiply_reduce_fusion
  558.0 183.7 %while.31 = (s32[]{:T(128)}, f32[128,16,64]{0,2,1:T(8,128)S(1)}, f32[2,512,16,64]{1,0,3,2:T(2,128)}, f32[2,512,16,64]{1,0,3,2:T(2,128)}, bf16[2,512,16,64]{1,3,2...) while((s32[]{:T(128)}, f32[128,16,64]{0,2,1:T(8,128)S(1)}, ...), condition=%wide.region_14.15_spmd.clone, body=%wide.region_13.14_spmd.clone.sunk | while | flops 682950656 | bytes 70482664 | solution.py:156
  568.5 38.1 %dynamic_update_slice.11 = f32[2,512,16,64]{1,0,3,2:T(2,128)} dynamic-update-slice(f32[2,512,16,64]{1,0,3,2:T(2,128)} %get-tuple-element.569, f32[1,512,16,64]{1,0,3,2:T(1,128)S(1)} %copy.146, s32[]{:T(128)S(6)} %copy.166, s32[]{:T(128)} %constant.108.clone.1..sunk.1, s32[]{:T(128)} %constant.108.clone.1..sunk.1, s32[]{:T(128)} %constant.108.clone.1..sunk.1) | dynamic-update-slice | bytes 4194308 | tf_op jit(solution)/shard_map/while/body/jit(dynamic_update_index_in_dim)/dynamic_update_slice | solution.py:156
  611.9 38.0 %dynamic_update_slice.12 = f32[2,512,16,64]{1,0,3,2:T(2,128)} dynamic-update-slice(f32[2,512,16,64]{1,0,3,2:T(2,128)} %get-tuple-element.570, f32[1,512,16,64]{1,0,3,2:T(1,128)S(1)} %copy.147, s32[]{:T(128)S(6)} %copy.166, s32[]{:T(128)} %constant.108.clone.1..sunk.1, s32[]{:T(128)} %constant.108.clone.1..sunk.1, s32[]{:T(128)} %constant.108.clone.1..sunk.1) | dynamic-update-slice | bytes 4194308 | tf_op jit(solution)/shard_map/while/body/jit(dynamic_update_index_in_dim)/dynamic_update_slice | solution.py:156
  660.2 38.1 %dynamic_update_slice.11 = f32[2,512,16,64]{1,0,3,2:T(2,128)} dynamic-update-slice(f32[2,512,16,64]{1,0,3,2:T(2,128)} %get-tuple-element.569, f32[1,512,16,64]{1,0,3,2:T(1,128)S(1)} %copy.146, s32[]{:T(128)S(6)} %copy.166, s32[]{:T(128)} %constant.108.clone.1..sunk.1, s32[]{:T(128)} %constant.108.clone.1..sunk.1, s32[]{:T(128)} %constant.108.clone.1..sunk.1) | dynamic-update-slice | bytes 4194308 | tf_op jit(solution)/shard_map/while/body/jit(dynamic_update_index_in_dim)/dynamic_update_slice | solution.py:156
  703.7 38.0 %dynamic_update_slice.12 = f32[2,512,16,64]{1,0,3,2:T(2,128)} dynamic-update-slice(f32[2,512,16,64]{1,0,3,2:T(2,128)} %get-tuple-element.570, f32[1,512,16,64]{1,0,3,2:T(1,128)S(1)} %copy.147, s32[]{:T(128)S(6)} %copy.166, s32[]{:T(128)} %constant.108.clone.1..sunk.1, s32[]{:T(128)} %constant.108.clone.1..sunk.1, s32[]{:T(128)} %constant.108.clone.1..sunk.1) | dynamic-update-slice | bytes 4194308 | tf_op jit(solution)/shard_map/while/body/jit(dynamic_update_index_in_dim)/dynamic_update_slice | solution.py:156
  754.7 41.8 %reduce-scatter.3.cloned.1.call-done = f32[128,1024]{0,1:T(8,128)} async-done(((f32[1024,1024]{0,1:T(8,128)}), f32[128,1024]{0,1:T(8,128)}) %reduce-scatter.3.cloned.1.call-update) | async-done | bytes 524304 | tf_op jit(solution)/shard_map/reduce_scatter | solution.py:158
  797.6 54.6 %reduce-scatter.5.cloned.1.call-done = f32[128,1024]{0,1:T(8,128)} async-done(((f32[1024,1024]{0,1:T(8,128)}), f32[128,1024]{0,1:T(8,128)}) %reduce-scatter.5.cloned.1.call-update) | async-done | bytes 524304 | tf_op jit(solution)/shard_map/reduce_scatter | solution.py:159
  861.1 14.2 %all-to-all-done.1 = bf16[128,4,256]{2,0,1:T(8,128)(2,1)S(1)} async-done(((bf16[128,4,256]{2,0,1:T(8,128)(2,1)}), bf16[128,4,256]{2,0,1:T(8,128)(2,1)S(1)}, u32[]{:S(2)}, u32[]{:S(2)}) %all-to-all-start.1) | async-done | bytes 262176 | tf_op jit(solution)/shard_map/all_to_all | solution.py:374
  880.4 34.8 %all-to-all-done.3 = bf16[128,4,1024]{2,0,1:T(8,128)(2,1)S(1)} async-done(((bf16[128,4,1024]{2,0,1:T(8,128)(2,1)}), bf16[128,4,1024]{2,0,1:T(8,128)(2,1)S(1)}, u32[]{:S(2)}, u32[]{:S(2)}) %all-to-all-start.3) | async-done | bytes 1048608 | tf_op jit(solution)/shard_map/all_to_all | solution.py:376
  937.0 74.6 %all-gather.32.cloned.1.call-done = bf16[512,4096]{1,0:T(8,128)(2,1)} async-done(((bf16[128,4096]{1,0:T(8,128)(2,1)}), bf16[512,4096]{1,0:T(8,128)(2,1)}) %all-gather.32.cloned.1.call-update) | async-done | bytes 4194320 | tf_op jit(solution)/shard_map/all_gather | solution.py:381
  1017.1 57.9 %all-gather.28.cloned.1.call-done = bf16[512,3072]{0,1:T(8,128)(2,1)} async-done(((bf16[128,3072]{0,1:T(8,128)(2,1)}), bf16[512,3072]{0,1:T(8,128)(2,1)}) %all-gather.28.cloned.1.call-update) | async-done | bytes 3145744 | tf_op jit(solution)/shard_map/all_gather | solution.py:379
  1080.2 8.0 all-gather.12
  1098.7 17.7 %all-reduce.11 = (f32[1024]{0:T(1024)S(1)}, f32[1024]{0:T(1024)S(1)}, f32[1024]{0:T(1024)S(1)}, f32[1024]{0:T(1024)S(1)}, f32[1024]{0:T(1024)S(1)}, /*index=5*/f...) all-reduce(f32[1024]{0:T(1024)S(1)} %get-tuple-element.289, ...), channel_id=17, replica_groups=mesh['ctx'=8,'fsdp'=4] {'fsdp'}, use_global_device_ids=true, to_apply=%region_20.21.clone | all-reduce | flops 12288 | bytes 98304
  1117.1 23.8 %all-reduce.9 = (f32[1,256]{1,0:T(1,128)}, f32[1,256]{1,0:T(1,128)}, f32[1,256]{1,0:T(1,128)}, f32[1,256]{1,0:T(1,128)}, f32[1,256]{1,0:T(1,128)}, /*index=5*/f3...) all-reduce(f32[1,256]{1,0:T(1,128)S(1)} %bitcast.312, ...), channel_id=1, replica_groups=mesh['ctx'=8,'fsdp'=4] {'ctx'}, use_global_device_ids=true, to_apply=%region_21.22 | all-reduce | flops 3072 | bytes 24576 | tf_op jit(solution)/shard_map/psum | solution.py:406
  1142.0 110.2 %all-reduce.14.cloned.1.call-done = (f32[1,256,3072]{2,1,0:T(8,128)}, f32[1,256,1024]{2,1,0:T(8,128)}, f32[1,256,4096]{2,1,0:T(8,128)}, f32[1,1024,1024]{2,1,0:T(8,128)}) async-done(((f32[1,256,3072]{2,1,0:T(8,128)}, f32[1,256,1024]{2,1,0:T(8,128)}, f32[1,256,4096]{2,1,0:T(8,128)}, f32[1,1024,1024]{2,1,0:T(8,128)}), (f32[1,256,3072]{2,1,0:T(8,128)}, f32[1,256,1024]{2,1,0:T(8,128)}, ...) | async-done | bytes 12582928 | tf_op jit(solution)/shard_map/psum | solution.py:406
  (242 shorter events, 167.1 us)
Async XLA Ops:
  7.2 120.5 %all-gather.36.cloned.1.call-start = ((), (), s32[]{:S(2)}) async-start(), calls=%async_computation.14 | async-start | bytes 7864320 | tf_op jit(solution)/shard_map/all_gather | solution.py:350
  7.9 183.3 %all-gather.24.cloned.1.call-start = ((), (), s32[]{:S(2)}) async-start(), calls=%async_computation.6 | async-start | bytes 2359296 | tf_op jit(solution)/shard_map/all_gather | solution.py:63
  132.5 70.6 %all-gather.26.cloned.1.call-start = ((), (), s32[]{:S(2)}) async-start(), calls=%async_computation.7 | async-start | bytes 2359296 | tf_op jit(solution)/shard_map/all_gather | solution.py:64
  149.7 23.9 %copy-start.32 = (bf16[1,256]{1,0:T(2,128)(2,1)S(1)}, bf16[1,256]{1,0:T(2,128)(2,1)}, u32[]{:S(2)}) copy-start(bf16[1,256]{1,0:T(2,128)(2,1)} %param.31) | copy-start | bytes 1540
  149.7 33.2 %copy-start.33 = (bf16[1,256]{1,0:T(2,128)(2,1)S(1)}, bf16[1,256]{1,0:T(2,128)(2,1)}, u32[]{:S(2)}) copy-start(bf16[1,256]{1,0:T(2,128)(2,1)} %param.30) | copy-start | bytes 1540
  149.7 41.2 %copy-start.14 = (f32[1,128,1024]{2,1,0:T(8,128)S(1)}, f32[1,128,1024]{2,1,0:T(8,128)}, u32[]{:S(2)}) copy-start(f32[1,128,1024]{2,1,0:T(8,128)} %param.21) | copy-start | bytes 1572868
  150.6 85.9 %all-gather.38.cloned.1.call-start = ((), (), s32[]{:S(2)}) async-start(), calls=%async_computation.15 | async-start | bytes 2621440 | tf_op jit(solution)/shard_map/all_gather | solution.py:353
  151.2 235.2 %all-gather.40.cloned.1.call-start = ((), (), s32[]{:S(2)}) async-start(), calls=%async_computation.16 | async-start | bytes 10485760 | tf_op jit(solution)/shard_map/all_gather | solution.py:357
  151.8 383.9 %all-gather.42.cloned.1.call-start = ((), (), s32[]{:S(2)}) async-start(), calls=%async_computation.17 | async-start | bytes 10485760 | tf_op jit(solution)/shard_map/all_gather | solution.py:359
  152.3 644.2 %reduce-scatter.3.cloned.1.call-start = ((), (), s32[]{:S(2)}) async-start(), calls=%async_computation.8 | async-start | bytes 4718592 | tf_op jit(solution)/shard_map/reduce_scatter | solution.py:158
  191.0 344.7 %copy-start.17 = (bf16[128,1024]{1,0:T(8,128)(2,1)}, bf16[128,1024]{1,0:T(8,128)(2,1)S(1)}, u32[]{:S(2)}) copy-start(bf16[128,1024]{1,0:T(8,128)(2,1)S(1)} %get-tuple-element.370) | copy-start | bytes 786436
  235.6 157.7 %copy-start.16 = (f32[128,16,64]{0,2,1:T(8,128)}, f32[128,16,64]{0,2,1:T(8,128)S(1)}, u32[]{:S(2)}) copy-start(f32[128,16,64]{0,2,1:T(8,128)S(1)} %get-tuple-element.128) | copy-start | bytes 1572868
  235.7 157.6 %copy-start.11 = (bf16[128,16,64]{0,2,1:T(8,128)(2,1)}, bf16[128,16,64]{0,2,1:T(8,128)(2,1)S(1)}, u32[]{:S(2)}) copy-start(bf16[128,16,64]{0,2,1:T(8,128)(2,1)S(1)} %divide_convert_fusion) | copy-start | bytes 786436
  239.1 154.2 %copy-start.20 = (bf16[128,1024]{1,0:T(8,128)(2,1)}, bf16[128,1024]{1,0:T(8,128)(2,1)S(1)}, u32[]{:S(2)}) copy-start(bf16[128,1024]{1,0:T(8,128)(2,1)S(1)} %add_convert_fusion) | copy-start | bytes 786436
  746.8 105.3 %reduce-scatter.5.cloned.1.call-start = ((), (), s32[]{:S(2)}) async-start(), calls=%async_computation.9 | async-start | bytes 4718592 | tf_op jit(solution)/shard_map/reduce_scatter | solution.py:159
  752.1 102.5 %copy-start.12 = (bf16[128,16,64]{0,2,1:T(8,128)(2,1)S(1)}, bf16[128,16,64]{0,2,1:T(8,128)(2,1)}, u32[]{:S(2)}) copy-start(bf16[128,16,64]{0,2,1:T(8,128)(2,1)} %copy-done.11) | copy-start | bytes 786436
  752.1 168.8 %all-gather.34.cloned.1.call-start = ((), (), s32[]{:S(2)}) async-start(), calls=%async_computation.13 | async-start | bytes 1310720 | tf_op jit(solution)/shard_map/all_gather | solution.py:382
  752.9 181.4 %all-gather.30.cloned.1.call-start = ((), (), s32[]{:S(2)}) async-start(), calls=%async_computation.11 | async-start | bytes 1310720 | tf_op jit(solution)/shard_map/all_gather | solution.py:380
  753.5 258.1 %all-gather.32.cloned.1.call-start = ((), (), s32[]{:S(2)}) async-start(), calls=%async_computation.12 | async-start | bytes 5242880 | tf_op jit(solution)/shard_map/all_gather | solution.py:381
  754.2 105.9 %copy-start.5 = (bf16[128,4096]{1,0:T(8,128)(2,1)S(1)}, bf16[128,4096]{1,0:T(8,128)(2,1)}, u32[]{:S(2)}) copy-start(bf16[128,4096]{1,0:T(8,128)(2,1)} %get-tuple-element.377) | copy-start | bytes 3145732
  754.2 320.8 %all-gather.28.cloned.1.call-start = ((), (), s32[]{:S(2)}) async-start(), calls=%async_computation.10 | async-start | bytes 3932160 | tf_op jit(solution)/shard_map/all_gather | solution.py:379
  754.7 99.8 %copy-start.22 = (bf16[128,16,64]{0,2,1:T(8,128)(2,1)}, bf16[128,16,64]{0,2,1:T(8,128)(2,1)S(1)}, u32[]{:S(2)}) copy-start(bf16[128,16,64]{0,2,1:T(8,128)(2,1)S(1)} %get-tuple-element.374) | copy-start | bytes 786436
  797.6 63.5 %copy-start.24 = (bf16[128,1024]{0,1:T(8,128)(2,1)}, bf16[128,1024]{0,1:T(8,128)(2,1)S(1)}, u32[]{:S(2)}) copy-start(bf16[128,1024]{0,1:T(8,128)(2,1)S(1)} %convert.16) | copy-start | bytes 786436
  853.6 21.7 %copy-start.26 = (bf16[128,1024]{0,1:T(8,128)(2,1)}, bf16[128,1024]{0,1:T(8,128)(2,1)S(1)}, u32[]{:S(2)}) copy-start(bf16[128,1024]{0,1:T(8,128)(2,1)S(1)} %get-tuple-element.372) | copy-start | bytes 786436
  854.6 24.8 %copy-start.3 = (bf16[1,128,1024]{2,1,0:T(8,128)(2,1)S(1)}, bf16[1,128,1024]{2,1,0:T(8,128)(2,1)}, u32[]{:S(2)}) copy-start(bf16[1,128,1024]{2,1,0:T(8,128)(2,1)} %param.20) | copy-start | bytes 786436
  854.6 25.1 %copy-start.21 = (bf16[128,1024]{1,0:T(8,128)(2,1)S(1)}, bf16[128,1024]{1,0:T(8,128)(2,1)}, u32[]{:S(2)}) copy-start(bf16[128,1024]{1,0:T(8,128)(2,1)} %copy-done.20) | copy-start | bytes 786436
  855.5 19.8 %all-to-all-start.1 = ((bf16[128,4,256]{2,0,1:T(8,128)(2,1)}), bf16[128,4,256]{2,0,1:T(8,128)(2,1)S(1)}, u32[]{:S(2)}, u32[]{:S(2)}) async-start(bf16[128,4,256]{2,0,1:T(8,128)(2,1)} %copy.94), calls=%async_computation.3 | async-start | bytes 524288 | tf_op jit(solution)/shard_map/all_to_all | solution.py:374
  875.3 39.9 %all-to-all-start.3 = ((bf16[128,4,1024]{2,0,1:T(8,128)(2,1)}), bf16[128,4,1024]{2,0,1:T(8,128)(2,1)S(1)}, u32[]{:S(2)}, u32[]{:S(2)}) async-start(bf16[128,4,1024]{2,0,1:T(8,128)(2,1)} %bitcast.224), calls=%async_computation.5 | async-start | bytes 2097152 | tf_op jit(solution)/shard_map/all_to_all | solution.py:376
  916.2 14.6 %all-to-all-start.2 = ((bf16[128,4,256]{2,0,1:T(8,128)(2,1)}), bf16[128,4,256]{2,0,1:T(8,128)(2,1)S(1)}, u32[]{:S(2)}, u32[]{:S(2)}) async-start(bf16[128,4,256]{2,0,1:T(8,128)(2,1)} %bitcast.225), calls=%async_computation.4 | async-start | bytes 524288 | tf_op jit(solution)/shard_map/all_to_all | solution.py:375
  930.8 86.3 %all-to-all-start = ((bf16[128,4,256]{2,0,1:T(8,128)(2,1)}), bf16[128,4,256]{2,0,1:T(8,128)(2,1)S(1)}, u32[]{:S(2)}, u32[]{:S(2)}) async-start(bf16[128,4,256]{2,0,1:T(8,128)(2,1)} %fusion.103), calls=%async_computation.2 | async-start | bytes 524288 | tf_op jit(solution)/shard_map/all_to_all | solution.py:373
  934.2 318.0 %all-reduce.14.cloned.1.call-start = ((), (), s32[]{:S(2)}) async-start(), calls=%async_computation.18 | async-start | bytes 25165824 | tf_op jit(solution)/shard_map/psum | solution.py:406
  1096.3 44.6 %copy-start.7 = (f32[128,1024]{1,0:T(8,128)S(1)}, f32[128,1024]{1,0:T(8,128)}, u32[]{:S(2)}) copy-start(f32[128,1024]{1,0:T(8,128)} %copy-done.6) | copy-start | bytes 1572868
  (27 other events, 155.3 us)
Sparse Core Ops, SparseCore 0:
  9.6 118.0 all-gather.35
  132.6 26.1 all-gather.23
  161.2 27.8 all-gather.25
  190.6 45.9 all-gather.37
  237.9 148.3 all-gather.39
  387.8 147.8 all-gather.41
  747.0 49.4 reduce-scatter.2
  800.8 51.3 reduce-scatter.4
  853.7 41.3 all-gather.33
  896.5 34.2 all-gather.29
  932.3 79.1 all-gather.31
  1013.0 61.9 all-gather.27
  1080.1 172.0 all-reduce.13
where the time goes:
time: 1290 us; the launch traced here: 1270 us
  waiting for transfers between devices  785 us (61%)
  local copies, waits for them, and re-layouts  216 us (17%)
  blocking collectives  126 us (10%)
  matrix products  90.9 us (7%)
  other arithmetic  18.8 us (1%)
  starting transfers between devices  16.6 us (1%)
  between operations  16.2 us (1%)
    dynamic_update_slice x8, local copies, waits for them, and re-layouts, back_keys(): lax.scan(back_one_block, zero_state, inputs_all)  161 us
    all_gather x1, waiting for transfers between devices, shards(): lax.all_gather(fc_weight[layer_idx], 'fsdp', axis=0, tiled=True)  147 us
    all_gather x1, waiting for transfers between devices, shards(): lax.all_gather(out_weight[layer_idx], 'fsdp', axis=0, tiled=True)  142 us
    psum x1, waiting for transfers between devices, shards(): lax.psum((shard_grads[0], shard_grads[1], shard_grads[2], shard_grads[3],...  110 us
    all_gather x1, waiting for transfers between devices, shards(): lax.all_gather(qkv_weight[layer_idx], 'fsdp', axis=0, tiled=True)  96.7 us
    all_gather x1, waiting for transfers between devices, shards(): lax.all_gather(row_pairs[2][1], 'fsdp', axis=0, tiled=True)  74.6 us
    all_gather x1, waiting for transfers between devices, shards(): lax.all_gather(row_pairs[0][1], 'fsdp', axis=0, tiled=True)  57.9 us
    reduce_scatter x1, waiting for transfers between devices, back_keys(): lax.psum_scatter(value_terms.reshape(total_rows, D), 'ctx', scatter_dimen...  54.6 us
  transfers between devices with their start and end apart: 17, of which 12 were waited for; matrix products, arithmetic and copies ran while one was open for 7% of the time, Pallas kernels for 0%

commit v1 on v0

v1 whole, which is shorter than its diff:
```python
import math

import jax
import jax.numpy as jnp
from jax import lax
from jax.experimental import pallas as pl
from jax.experimental.pallas import tpu as pltpu
from jax.sharding import Mesh
from jax.sharding import PartitionSpec as P

D = 1024
HEADS = 16
HEAD_DIM = 64
LAYERS = 1
CTX = ("chip", "core")


NORM_EPS = 1e-05
GELU_SCALE = math.sqrt(2.0 / math.pi)


def layer_norm(values_in, gain_vec, shift_vec):
    center = values_in - jnp.mean(values_in, axis=-1, keepdims=True)
    variance = jnp.mean(center * center, axis=-1, keepdims=True)
    inverse = lax.rsqrt(variance + NORM_EPS)
    normed = center * inverse
    return (normed * gain_vec + shift_vec, normed, inverse)


def norm_back(upstream, normed, inverse, gain_vec):
    scaled = upstream * gain_vec
    inner_term = (
        scaled
        - jnp.mean(scaled, axis=-1, keepdims=True)
        - normed * jnp.mean(scaled * normed, axis=-1, keepdims=True)
    )
    return (inverse * inner_term, jnp.sum(upstream * normed, axis=0), jnp.sum(upstream, axis=0))


def gelu_pair(pre_act):
    inner_arg = GELU_SCALE * (pre_act + 0.044715 * pre_act * pre_act * pre_act)
    tangent = jnp.tanh(inner_arg)
    output = 0.5 * pre_act * (1.0 + tangent)
    gelu_slope = 0.5 * (1.0 + tangent) + 0.5 * pre_act * (1.0 - tangent * tangent) * GELU_SCALE * (
        1.0 + 3.0 * 0.044715 * pre_act * pre_act
    )
    return (output, gelu_slope)


def token_positions(order_row, row_total, half_block):
    slots = order_row.shape[0]
    return (order_row[:, None] * half_block + jnp.arange(half_block, dtype=jnp.int32)).reshape(
        slots * half_block
    )


def dot_nt(left, right):
    return lax.dot_general(left, right, (((1,), (1,)), ((), ())), preferred_element_type=jnp.float32)


def dot_tn(left, right):
    return lax.dot_general(left, right, (((0,), (0,)), ((), ())), preferred_element_type=jnp.float32)


def attend_kernel(q_ref, k_ref, v_ref, qpos_ref, kpos_ref, out_ref, lse_ref):
    allowed = kpos_ref[...] <= qpos_ref[...]
    heads = q_ref.shape[1] // HEAD_DIM
    outs, lses = [], []
    for h in range(heads):
        cols = slice(h * HEAD_DIM, (h + 1) * HEAD_DIM)
        scores = dot_nt(q_ref[:, cols], k_ref[:, cols]) * 0.125
        scores = jnp.where(allowed, scores, -1e30)
        top = jnp.max(scores, axis=1, keepdims=True)
        probs = jnp.exp(scores - top)
        total = jnp.sum(probs, axis=1, keepdims=True)
        acc = jnp.dot(probs.astype(jnp.bfloat16), v_ref[:, cols], preferred_element_type=jnp.float32)
        outs.append((acc / total).astype(jnp.bfloat16))
        lses.append(top + jnp.log(total))
    out_ref[...] = jnp.concatenate(outs, axis=1) if heads > 1 else outs[0]
    lse_ref[...] = jnp.concatenate(lses, axis=1) if heads > 1 else lses[0]


def attend_back_kernel(
    q_ref, k_ref, v_ref, qpos_ref, kpos_ref, out_ref, grad_ref, lse_ref, dq_ref, dk_ref, dv_ref
):
    step = pl.program_id(0)
    allowed = kpos_ref[...] <= qpos_ref[...]
    heads = q_ref.shape[1] // HEAD_DIM
    dqs, dks, dvs = [], [], []
    for h in range(heads):
        cols = slice(h * HEAD_DIM, (h + 1) * HEAD_DIM)
        queries, keys, values, grads = q_ref[:, cols], k_ref[:, cols], v_ref[:, cols], grad_ref[:, cols]
        delta = jnp.sum(
            grads.astype(jnp.float32) * out_ref[:, cols].astype(jnp.float32), axis=1, keepdims=True
        )
        scores = dot_nt(queries, keys) * 0.125
        probs = jnp.exp(jnp.where(allowed, scores - lse_ref[:, h : h + 1], -1e30))
        grad_scores = (probs * (dot_nt(grads, values) - delta) * 0.125).astype(jnp.bfloat16)
        dvs.append(dot_tn(probs.astype(jnp.bfloat16), grads))
        dqs.append(jnp.dot(grad_scores, keys, preferred_element_type=jnp.float32))
        dks.append(dot_tn(grad_scores, queries))
    join = lambda parts: jnp.concatenate(parts, axis=1) if heads > 1 else parts[0]
    dq_ref[...] = join(dqs)

    @pl.when(step == 0)
    def _():
        dk_ref[...] = join(dks)
        dv_ref[...] = join(dvs)

    @pl.when(step > 0)
    def _():
        dk_ref[...] += join(dks)
        dv_ref[...] += join(dvs)


def attention_specs(total, width, heads, tile):
    row = pl.BlockSpec((tile, width), lambda i: (i, 0))
    full = pl.BlockSpec((total, width), lambda i: (0, 0))
    qpos = pl.BlockSpec((tile, 1), lambda i: (i, 0))
    kpos = pl.BlockSpec((1, total), lambda i: (0, 0))
    lse = pl.BlockSpec((tile, heads), lambda i: (i, 0))
    return row, full, qpos, kpos, lse


def run_attend(queries, keys, values, position):
    total, width = queries.shape
    heads = width // HEAD_DIM
    tile = 256
    row, full, qpos, kpos, lse = attention_specs(total, width, heads, tile)
    return pl.pallas_call(
        attend_kernel,
        grid=(total // tile,),
        in_specs=[row, full, full, qpos, kpos],
        out_specs=[row, lse],
        out_shape=[
            jax.ShapeDtypeStruct((total, width), jnp.bfloat16),
            jax.ShapeDtypeStruct((total, heads), jnp.float32),
        ],
        compiler_params=pltpu.CompilerParams(vmem_limit_bytes=40 * 1024 * 1024),
        cost_estimate=pl.CostEstimate(
            flops=4 * total * total * width, bytes_accessed=8 * total * width, transcendentals=total * total * heads
        ),
    )(queries, keys, values, position[:, None], position[None, :])


def run_attend_back(queries, keys, values, position, att_out, grad_att, lse_rows):
    total, width = queries.shape
    heads = width // HEAD_DIM
    tile = 256
    row, full, qpos, kpos, lse = attention_specs(total, width, heads, tile)
    shape = jax.ShapeDtypeStruct((total, width), jnp.float32)
    return pl.pallas_call(
        attend_back_kernel,
        grid=(total // tile,),
        in_specs=[row, full, full, qpos, kpos, row, row, lse],
        out_specs=[row, full, full],
        out_shape=[shape, shape, shape],
        compiler_params=pltpu.CompilerParams(vmem_limit_bytes=40 * 1024 * 1024),
        cost_estimate=pl.CostEstimate(
            flops=10 * total * total * width, bytes_accessed=22 * total * width, transcendentals=total * total * heads
        ),
    )(queries, keys, values, position[:, None], position[None, :], att_out, grad_att, lse_rows)


def swap_cores(rows):
    return lax.ppermute(rows, "core", [(0, 1), (1, 0)])


def to_heads(rows, parts):
    count = rows.shape[0]
    n = lax.axis_size(CTX)
    width = D // n
    stacked = rows.reshape(count, parts, n, width).transpose(2, 0, 1, 3).reshape(n, count, parts * width)
    moved = lax.all_to_all(stacked, CTX, split_axis=0, concat_axis=0, tiled=True)
    moved = moved.reshape(n * count, parts * width)
    return tuple(moved[:, p * width : (p + 1) * width] for p in range(parts))


def to_tokens(columns):
    parts = len(columns)
    n = lax.axis_size(CTX)
    total, width = columns[0].shape
    count = total // n
    joined = jnp.concatenate(columns, axis=1).reshape(n, count, parts * width)
    moved = lax.all_to_all(joined, CTX, split_axis=0, concat_axis=0, tiled=True)
    return moved.reshape(n, count, parts, width).transpose(1, 2, 0, 3).reshape(count, parts * n * width)


def layer_forward(stream, weights_now, position):
    (
        gain_one,
        shift_one,
        qkv_w,
        query_b,
        value_b,
        proj_w,
        proj_b,
        gain_two,
        shift_two,
        fc_w,
        fc_b,
        out_w,
        out_b,
    ) = weights_now
    normed_out, normed_one, inverse_one = layer_norm(
        stream, gain_one.astype(jnp.float32), shift_one.astype(jnp.float32)
    )
    attn_in = normed_out.astype(jnp.bfloat16)
    projected = jnp.dot(attn_in, qkv_w, preferred_element_type=jnp.float32)
    bias_row = jnp.concatenate([query_b, jnp.zeros_like(query_b), value_b]).astype(jnp.float32)
    qkv_rows = (projected + bias_row).astype(jnp.bfloat16)
    queries, key_rows, value_rows = to_heads(qkv_rows, 3)
    att_heads, lse_rows = run_attend(queries, key_rows, value_rows, position)
    att_out = to_tokens((att_heads,))
    middle = (
        stream
        + jnp.dot(att_out, proj_w, preferred_element_type=jnp.float32)
        + proj_b.astype(jnp.float32)
    )
    normed_mid, normed_two, inverse_two = layer_norm(
        middle, gain_two.astype(jnp.float32), shift_two.astype(jnp.float32)
    )
    mlp_in = normed_mid.astype(jnp.bfloat16)
    pre_act = jnp.dot(mlp_in, fc_w, preferred_element_type=jnp.float32) + fc_b.astype(jnp.float32)
    activated, gelu_slope = gelu_pair(pre_act)
    act_rows = activated.astype(jnp.bfloat16)
    result = (
        middle
        + jnp.dot(act_rows, out_w, preferred_element_type=jnp.float32)
        + out_b.astype(jnp.float32)
    )
    record = (
        normed_one,
        inverse_one,
        attn_in,
        queries,
        key_rows,
        value_rows,
        att_heads,
        att_out,
        lse_rows,
        normed_two,
        inverse_two,
        mlp_in,
        gelu_slope,
        act_rows,
    )
    return (result, record)


def layer_backward(upstream, weights_now, record, position):
    (
        gain_one,
        shift_one,
        qkv_w,
        query_b,
        value_b,
        proj_w,
        proj_b,
        gain_two,
        shift_two,
        fc_w,
        fc_b,
        out_w,
        out_b,
    ) = weights_now
    (
        normed_one,
        inverse_one,
        attn_in,
        queries,
        key_rows,
        value_rows,
        att_heads,
        att_out,
        lse_rows,
        normed_two,
        inverse_two,
        mlp_in,
        gelu_slope,
        act_rows,
    ) = record
    up_rows = upstream.astype(jnp.bfloat16)
    grad_out_b = jnp.sum(upstream, axis=0)
    grad_act = jnp.dot(up_rows, out_w.T, preferred_element_type=jnp.float32)
    grad_pre = grad_act * gelu_slope
    grad_pre_rows = grad_pre.astype(jnp.bfloat16)
    grad_fc_b = jnp.sum(grad_pre, axis=0)
    grad_mlp_in = jnp.dot(grad_pre_rows, fc_w.T, preferred_element_type=jnp.float32)
    back_two, grad_gain_two, grad_shift_two = norm_back(
        grad_mlp_in, normed_two, inverse_two, gain_two.astype(jnp.float32)
    )
    mid_grad = upstream + back_two
    mid_rows = mid_grad.astype(jnp.bfloat16)
    grad_proj_b = jnp.sum(mid_grad, axis=0)
    grad_att = jnp.dot(mid_rows, proj_w.T, preferred_element_type=jnp.float32).astype(jnp.bfloat16)
    (grad_heads,) = to_heads(grad_att, 1)
    grad_query, grad_key, grad_value = run_attend_back(
        queries, key_rows, value_rows, position, att_heads, grad_heads, lse_rows
    )
    head_sums = jnp.stack([jnp.sum(grad_query, axis=0), jnp.sum(grad_value, axis=0)])
    mine = lax.axis_index(CTX) * head_sums.shape[1]
    spread = lax.dynamic_update_slice(jnp.zeros((2, D), jnp.float32), head_sums, (0, mine))
    grad_query_b, grad_value_b = spread[0], spread[1]
    grad_qkv_rows = to_tokens(
        tuple(part.astype(jnp.bfloat16) for part in (grad_query, grad_key, grad_value))
    )
    grad_attn_in = jnp.dot(grad_qkv_rows, qkv_w.T, preferred_element_type=jnp.float32)
    back_one, grad_gain_one, grad_shift_one = norm_back(
        grad_attn_in, normed_one, inverse_one, gain_one.astype(jnp.float32)
    )
    new_upstream = mid_grad + back_one
    vectors = (
        grad_gain_one,
        grad_shift_one,
        grad_query_b,
        grad_value_b,
        grad_proj_b,
        grad_gain_two,
        grad_shift_two,
        grad_fc_b,
        grad_out_b,
    )
    row_pairs = (
        (attn_in, grad_qkv_rows),
        (att_out, mid_rows),
        (mlp_in, grad_pre_rows),
        (act_rows, up_rows),
    )
    return (new_upstream, vectors, row_pairs)


def assemble(vectors, matrices):
    return (
        vectors[0],
        vectors[1],
        matrices[0],
        vectors[2],
        vectors[3],
        matrices[1],
        vectors[4],
        vectors[5],
        vectors[6],
        matrices[2],
        vectors[7],
        matrices[3],
        vectors[8],
    )


def shards(
    tokens,
    cotangent,
    block_order,
    ln1_gain,
    ln1_bias,
    qkv_weight,
    query_bias,
    value_bias,
    proj_weight,
    proj_bias,
    ln2_gain,
    ln2_bias,
    fc_weight,
    fc_bias,
    out_weight,
    out_bias,
):
    row_count = tokens.shape[1]
    contexts = lax.axis_size(CTX)
    groups = lax.axis_size("fsdp")
    slots = block_order.shape[1]
    half_block = row_count * contexts // slots
    position = token_positions(block_order[0], row_count * contexts, half_block)
    stream = tokens[0].astype(jnp.float32)
    vectors_in = (
        ln1_gain, ln1_bias, query_bias, value_bias, proj_bias, ln2_gain, ln2_bias, fc_bias, out_bias,
    )
    sizes = [v.shape[1] for v in vectors_in]
    gathered = lax.all_gather(jnp.concatenate([v[0] for v in vectors_in]), "fsdp", axis=0)
    gathered_vectors = []
    start = 0
    for size in sizes:
        gathered_vectors.append(gathered[:, start : start + size].reshape(groups * size))
        start += size
    me = lax.axis_index(CTX)

    def gather_weight(weight):
        rows = weight.shape[1] // contexts
        piece = lax.dynamic_slice_in_dim(weight[0], me * rows, rows, axis=0)
        return lax.all_gather(piece, ("fsdp",) + CTX, axis=0, tiled=True)

    qkv_full = gather_weight(qkv_weight)
    proj_full = gather_weight(proj_weight)
    fc_full = gather_weight(fc_weight)
    out_full = gather_weight(out_weight)
    g = gathered_vectors
    full_weights = (
        g[0], g[1], qkv_full, g[2], g[3], proj_full, g[4], g[5], g[6], fc_full, g[7], out_full, g[8],
    )
    stream, record = layer_forward(stream, full_weights, position)
    upstream, vectors, row_pairs = layer_backward(cotangent[0], full_weights, record, position)
    matrices = []
    for left, right in row_pairs:
        features = left.shape[1] // (groups * 2)
        pieces = left.reshape(row_count, groups, 2, features)
        pieces = pieces.transpose(2, 0, 1, 3).reshape(2, row_count, groups * features)
        core = lax.axis_index("core")
        own_half = lax.dynamic_index_in_dim(pieces, core, 0, keepdims=False)
        sent_half = lax.dynamic_index_in_dim(pieces, 1 - core, 0, keepdims=False)
        left_half = jnp.concatenate([own_half, swap_cores(sent_half)])
        right_pair = jnp.concatenate([right, swap_cores(right)])
        terms = dot_tn(left_half, right_pair).astype(jnp.bfloat16)
        part = lax.psum_scatter(terms, ("fsdp", "chip"), scatter_dimension=0, tiled=True)
        total = lax.all_gather(part, ("core", "chip"), axis=0, tiled=True)
        matrices.append(total.astype(jnp.float32)[None])
    packed = jnp.concatenate([v.reshape(groups, -1) for v in vectors], axis=1)
    summed = lax.psum(packed, ("fsdp",) + CTX)
    own = lax.dynamic_index_in_dim(summed, lax.axis_index("fsdp"), 0, keepdims=True)
    vector_parts = []
    start = 0
    for v in vectors:
        size = v.shape[0] // groups
        vector_parts.append(own[:, start : start + size])
        start += size
    return (stream[None], upstream[None]) + assemble(vector_parts, matrices)


def solution(mesh):
    contexts, groups = mesh.devices.shape
    split_mesh = Mesh(mesh.devices.reshape(contexts // 2, 2, groups), ("chip", "core", "fsdp"))
    placed = (
        P("fsdp", CTX, None),
        P("fsdp", CTX, None),
        P("fsdp", None),
        P(None, "fsdp"),
        P(None, "fsdp"),
        P(None, "fsdp", None),
        P(None, "fsdp"),
        P(None, "fsdp"),
        P(None, "fsdp", None),
        P(None, "fsdp"),
        P(None, "fsdp"),
        P(None, "fsdp"),
        P(None, "fsdp", None),
        P(None, "fsdp"),
        P(None, "fsdp", None),
        P(None, "fsdp"),
    )
    return jax.shard_map(
        shards,
        mesh=split_mesh,
        in_specs=placed,
        out_specs=(
            P("fsdp", CTX, None),
            P("fsdp", CTX, None),
            P(None, "fsdp"),
            P(None, "fsdp"),
            P(None, "fsdp", None),
            P(None, "fsdp"),
            P(None, "fsdp"),
            P(None, "fsdp", None),
            P(None, "fsdp"),
            P(None, "fsdp"),
            P(None, "fsdp"),
            P(None, "fsdp", None),
            P(None, "fsdp"),
            P(None, "fsdp", None),
            P(None, "fsdp"),
        ),
        check_vma=False,
    )
```

time: 1290 us -> 858 us (0.67); the launches traced: 1270 us -> 857 us
  local copies, waits for them, and re-layouts: 216 us -> 24.9 us
  waiting for transfers between devices: 785 us -> 622 us
  matrix products: 90.9 us -> 48.6 us
  blocking collectives: 126 us -> 105 us
  Pallas kernels: 0 us -> 14.7 us
    all_gather x10 -> x7, waiting for transfers between devices: 520 us -> 279 us  [the longest x4 227 us: gather_weight(): return lax.all_gather(piece, ('fsdp',) + CTX, axis=0, tiled=True)]
    reduce_scatter x2 -> x4, waiting for transfers between devices: 96.4 us -> 325 us  [shards(): lax.psum_scatter(terms, ('fsdp', 'chip'), scatter_dimension=0, tiled=True)]
    dynamic_update_slice x8 -> x0, local copies, waits for them, and re-layouts: 161 us -> none  [back_keys(): lax.scan(back_one_block, zero_state, inputs_all)]
    psum x1 -> x0, waiting for transfers between devices: 110 us -> none  [shards(): lax.psum((shard_grads[0], shard_grads[1], shard_grads[2], shard_grads[3],...]
    all_gather x9 -> x2, blocking collectives: 84.1 us -> 40.9 us  [the longest x1 26.1 us: shards(): total = lax.all_gather(part, ('core', 'chip'), axis=0, tiled=True)]
    all_to_all x4 -> x2, waiting for transfers between devices: 54 us -> 12.4 us  [the longest x1 12.4 us: to_heads(): lax.all_to_all(stacked, CTX, split_axis=0, concat_axis=0, tiled=True)]
    dot_general x18 -> x4, matrix products: 53 us -> 13.3 us  [dot_tn(): lax.dot_general(left, right, (((0,), (0,)), ((), ())), preferred_element_...]
    unnamed x90 -> x77, local copies, waits for them, and re-layouts: 36.8 us -> 5.99 us
  transfers between devices with their start and end apart: 17 -> 21, of which waited for: 12 -> 16; matrix products, arithmetic and copies ran while one was open for 7% -> 8% of each run, Pallas kernels for 0% -> 1%
where the time goes in v1:
time: 858 us; the launch traced here: 857 us
  waiting for transfers between devices  622 us (72%)
  blocking collectives  105 us (12%)
  matrix products  48.6 us (6%)
  local copies, waits for them, and re-layouts  24.9 us (3%)
  other arithmetic  17.3 us (2%)
  Pallas kernels  14.7 us (2%)
  between operations  14.6 us (2%)
  starting transfers between devices  10.2 us (1%)
    reduce_scatter x4, waiting for transfers between devices, shards(): lax.psum_scatter(terms, ('fsdp', 'chip'), scatter_dimension=0, tiled=True)  325 us
    all_gather x4, waiting for transfers between devices, gather_weight(): return lax.all_gather(piece, ('fsdp',) + CTX, axis=0, tiled=True)  227 us
    all_gather x3, waiting for transfers between devices, shards(): total = lax.all_gather(part, ('core', 'chip'), axis=0, tiled=True)  51.7 us
    psum x1, blocking collectives, shards(): summed = lax.psum(packed, ('fsdp',) + CTX)  39.6 us
    all_gather x1, blocking collectives, shards(): total = lax.all_gather(part, ('core', 'chip'), axis=0, tiled=True)  26.1 us
  transfers between devices with their start and end apart: 21, of which 16 were waited for; matrix products, arithmetic and copies ran while one was open for 8% of the time, Pallas kernels for 1%

profile of v1, /device:TPU:0, one launch (start us, length us, event | category | flops | bytes accessed | tf_op | source)
XLA Modules:
  0.0 857.2 jit_solution(18340890613766492632)
XLA Ops:
  15.4 14.8 %all-gather = bf16[12288]{0:T(1024)(128)(2,1)S(1)} all-gather(bf16[3072]{0:T(1024)(128)(2,1)S(1)} %dynamic-update-slice.17), channel_id=2, replica_groups=mesh['chip'=4,'core'=2,'fsdp'=4] {'fsdp'}, dimensions={0}, use_global_device_ids=true | all-gather | bytes 30720 | tf_op jit(solution)/shard_map/all_gather | solution.py:380
  30.7 53.2 %all-gather.19.cloned.1.call-done = bf16[1,1024,3072]{2,1,0:T(8,128)(2,1)} async-done(((bf16[1,32,3072]{2,1,0:T(8,128)(2,1)}), bf16[1,1024,3072]{2,1,0:T(8,128)(2,1)}) %all-gather.19.cloned.1.call-update) | async-done | bytes 6291472 | tf_op jit(solution)/shard_map/all_gather | solution.py:391
  83.8 3.9 fusion.42
  89.3 3.5 all-to-all-start
  93.5 12.4 %all-to-all-done = bf16[8,128,384]{1,2,0:T(8,128)(2,1)S(1)} async-done(((bf16[8,128,384]{1,2,0:T(8,128)(2,1)}), bf16[8,128,384]{1,2,0:T(8,128)(2,1)S(1)}, u32[]{:S(2)}, u32[]{:S(2)}) %all-to-all-start) | async-done | bytes 786464 | tf_op jit(solution)/shard_map/all_to_all | solution.py:174
  106.4 5.6 shard_map.271
  112.9 3.4 all-to-all-start.1
  117.3 25.2 %all-gather.21.cloned.1.call-done = bf16[1,1024,1024]{2,1,0:T(8,128)(2,1)} async-done(((bf16[1,32,1024]{2,1,0:T(8,128)(2,1)}), bf16[1,1024,1024]{2,1,0:T(8,128)(2,1)}) %all-gather.21.cloned.1.call-update) | async-done | bytes 2097168 | tf_op jit(solution)/shard_map/all_gather | solution.py:391
  145.8 76.5 %all-gather.23.cloned.1.call-done = bf16[1,1024,4096]{2,1,0:T(8,128)(2,1)} async-done(((bf16[1,32,4096]{2,1,0:T(8,128)(2,1)}), bf16[1,1024,4096]{2,1,0:T(8,128)(2,1)}) %all-gather.23.cloned.1.call-update) | async-done | bytes 8388624 | tf_op jit(solution)/shard_map/all_gather | solution.py:391
  222.3 7.0 multiply_convert_fusion
  229.3 72.3 %all-gather.25.cloned.1.call-done = bf16[1,4096,1024]{2,1,0:T(8,128)(2,1)} async-done(((bf16[1,128,1024]{2,1,0:T(8,128)(2,1)}), bf16[1,4096,1024]{2,1,0:T(8,128)(2,1)}) %all-gather.25.cloned.1.call-update) | async-done | bytes 8388624 | tf_op jit(solution)/shard_map/all_gather | solution.py:391
  301.7 7.7 fusion.94
  315.2 9.5 %all_to_all.20 = bf16[8,128,128]{2,1,0:T(8,128)(2,1)S(1)} all-to-all(bf16[8,128,128]{2,1,0:T(8,128)(2,1)S(1)} %bitcast.216), channel_id=1, replica_groups=mesh['chip'=4,'core'=2,'fsdp'=4] {'chip','core'}, dimensions={0} | all-to-all | bytes 524288 | tf_op jit(solution)/shard_map/all_to_all | solution.py:174
  324.7 9.1 %shard_map.272 = (f32[1024,128]{1,0:T(8,128)S(1)}, f32[1024,128]{1,0:T(8,128)S(1)}, f32[1024,128]{1,0:T(8,128)S(1)}) custom-call(bf16[1024,128]{1,0:T(8,128)(2,1)S(1)} %get-tuple-element.43.q_ref, bf16[1024,128]{1,0:T(8,128)(2,1)S(1)} %get-tuple-element.42.k_ref, bf16[1024,128]{1,0:T(8,128)(2,1)S(1)} %get-tuple-element.41.v_ref, ...), custom_call_target="tpu_custom_call" | custom-call | flops 1342177280 | bytes 2883584 | tf_op jit(solution)/shard_map/pallas_call | solution.py:152
  334.5 15.0 %all_to_all.21 = bf16[8,128,384]{1,2,0:T(8,128)(2,1)S(1)} all-to-all(bf16[8,128,384]{1,2,0:T(8,128)(2,1)S(1)} %copy.51), channel_id=1, replica_groups=mesh['chip'=4,'core'=2,'fsdp'=4] {'chip','core'}, dimensions={0} | all-to-all | bytes 1572864 | tf_op jit(solution)/shard_map/all_to_all | solution.py:185
  352.3 3.8 convolution_convert_fusion.1
  358.9 3.7 copy.56
  366.3 3.3 convolution_convert_fusion.2
  372.7 4.9 convolution_convert_fusion
  381.8 103.1 %reduce-scatter.5.cloned.1.call-done = bf16[32,3072]{1,0:T(8,128)(2,1)} async-done(((bf16[512,3072]{1,0:T(8,128)(2,1)}), bf16[32,3072]{1,0:T(8,128)(2,1)}) %reduce-scatter.5.cloned.1.call-update) | async-done | bytes 196624 | tf_op jit(solution)/shard_map/reduce_scatter | solution.py:414
  484.9 97.0 %reduce-scatter.11.cloned.1.call-done = bf16[128,1024]{1,0:T(8,128)(2,1)} async-done(((bf16[2048,1024]{1,0:T(8,128)(2,1)}), bf16[128,1024]{1,0:T(8,128)(2,1)}) %reduce-scatter.11.cloned.1.call-update) | async-done | bytes 262160 | tf_op jit(solution)/shard_map/reduce_scatter | solution.py:414
  582.1 5.4 fusion.57
  587.6 91.9 %reduce-scatter.9.cloned.1.call-done = bf16[32,4096]{1,0:T(8,128)(2,1)} async-done(((bf16[512,4096]{1,0:T(8,128)(2,1)}), bf16[32,4096]{1,0:T(8,128)(2,1)}) %reduce-scatter.9.cloned.1.call-update) | async-done | bytes 262160 | tf_op jit(solution)/shard_map/reduce_scatter | solution.py:414
  679.5 5.2 multiply_reduce_fusion.1
  684.9 39.6 %psum.7 = f32[4,3072]{1,0:T(4,128)S(1)} all-reduce(f32[4,3072]{1,0:T(4,128)S(1)} %constant_dynamic-update-slice_fusion), channel_id=1, replica_groups=mesh['chip'=4,'core'=2,'fsdp'=4] {'fsdp','chip','core'}, use_global_device_ids=true, to_apply=%region_17.18 | all-reduce | flops 12288 | bytes 98304 | tf_op jit(solution)/shard_map/psum | solution.py:418
  726.9 33.0 %reduce-scatter.7.cloned.1.call-done = bf16[32,1024]{1,0:T(8,128)(2,1)} async-done(((bf16[512,1024]{1,0:T(8,128)(2,1)}), bf16[32,1024]{1,0:T(8,128)(2,1)}) %reduce-scatter.7.cloned.1.call-update) | async-done | bytes 65552 | tf_op jit(solution)/shard_map/reduce_scatter | solution.py:414
  760.0 26.1 %all_gather.37 = bf16[256,1024]{1,0:T(8,128)(2,1)S(1)} all-gather(bf16[32,1024]{1,0:T(8,128)(2,1)} %reduce-scatter.7.cloned.1.call-done), channel_id=1, replica_groups=mesh['chip'=4,'core'=2,'fsdp'=4] {'core','chip'}, dimensions={0}, use_global_device_ids=true | all-gather | bytes 589824 | tf_op jit(solution)/shard_map/all_gather | solution.py:415
  787.1 3.4 bitcast_convert_fusion.2
  790.6 26.0 %all-gather.17.cloned.1.call-done = bf16[1024,1024]{1,0:T(8,128)(2,1)} async-done(((bf16[128,1024]{1,0:T(8,128)(2,1)}), bf16[1024,1024]{1,0:T(8,128)(2,1)}) %all-gather.17.cloned.1.call-update) | async-done | bytes 2097168 | tf_op jit(solution)/shard_map/all_gather | solution.py:415
  816.6 4.2 bitcast_convert_fusion
  820.8 25.8 %all-gather.15.cloned.1.call-done = bf16[256,4096]{1,0:T(8,128)(2,1)} async-done(((bf16[32,4096]{1,0:T(8,128)(2,1)}), bf16[256,4096]{1,0:T(8,128)(2,1)}) %all-gather.15.cloned.1.call-update) | async-done | bytes 2097168 | tf_op jit(solution)/shard_map/all_gather | solution.py:415
  846.5 4.1 bitcast_convert_fusion.1
  (198 shorter events, 42.9 us)
Async XLA Ops:
  7.2 6.1 copy-start.20
  7.3 6.2 copy-start.21
  7.3 6.2 copy-start.22
  7.3 6.2 copy-start.15
  7.3 6.2 copy-start.23
  7.3 23.0 %copy-start.2 = (bf16[1,128,1024]{2,1,0:T(8,128)(2,1)S(1)}, bf16[1,128,1024]{2,1,0:T(8,128)(2,1)}, u32[]{:S(2)}) copy-start(bf16[1,128,1024]{2,1,0:T(8,128)(2,1)} %param.16) | copy-start | bytes 786436
  7.3 76.5 %all-gather.19.cloned.1.call-start = ((), (), s32[]{:S(2)}) async-start(), calls=%async_computation.15 | async-start | bytes 6488064 | tf_op jit(solution)/shard_map/all_gather | solution.py:391
  9.1 133.4 %all-gather.21.cloned.1.call-start = ((), (), s32[]{:S(2)}) async-start(), calls=%async_computation.16 | async-start | bytes 2162688 | tf_op jit(solution)/shard_map/all_gather | solution.py:391
  10.7 211.6 %all-gather.23.cloned.1.call-start = ((), (), s32[]{:S(2)}) async-start(), calls=%async_computation.17 | async-start | bytes 8650752 | tf_op jit(solution)/shard_map/all_gather | solution.py:391
  11.5 290.2 %all-gather.25.cloned.1.call-start = ((), (), s32[]{:S(2)}) async-start(), calls=%async_computation.18 | async-start | bytes 8650752 | tf_op jit(solution)/shard_map/all_gather | solution.py:391
  89.3 16.6 %all-to-all-start = ((bf16[8,128,384]{1,2,0:T(8,128)(2,1)}), bf16[8,128,384]{1,2,0:T(8,128)(2,1)S(1)}, u32[]{:S(2)}, u32[]{:S(2)}) async-start(bf16[8,128,384]{1,2,0:T(8,128)(2,1)} %bitcast.3), calls=%async_computation | async-start | bytes 1572864 | tf_op jit(solution)/shard_map/all_to_all | solution.py:174
  106.4 10.2 %copy-start.9 = (f32[1,128,1024]{2,1,0:T(8,128)S(1)}, f32[1,128,1024]{2,1,0:T(8,128)}, u32[]{:S(2)}) copy-start(f32[1,128,1024]{2,1,0:T(8,128)} %param.17) | copy-start | bytes 1572868
  112.9 29.7 %all-to-all-start.1 = ((bf16[8,128,128]{1,2,0:T(8,128)(2,1)}), bf16[8,128,128]{1,2,0:T(8,128)(2,1)S(1)}, u32[]{:S(2)}, u32[]{:S(2)}) async-start(bf16[8,128,128]{1,2,0:T(8,128)(2,1)} %copy.48), calls=%async_computation.1 | async-start | bytes 524288 | tf_op jit(solution)/shard_map/all_to_all | solution.py:185
  116.3 368.6 %reduce-scatter.5.cloned.1.call-start = ((), (), s32[]{:S(2)}) async-start(), calls=%async_computation.8 | async-start | bytes 3342336 | tf_op jit(solution)/shard_map/reduce_scatter | solution.py:414
  301.7 7.7 copy-start.4
  314.3 10.4 %copy-start.11 = (bf16[128,1024]{1,0:T(8,128)(2,1)}, bf16[128,1024]{1,0:T(8,128)(2,1)S(1)}, u32[]{:S(2)}) copy-start(bf16[128,1024]{1,0:T(8,128)(2,1)S(1)} %convert_element_type.178) | copy-start | bytes 786436
  349.5 2.8 collective-permute-start.1
  350.8 1.5 collective-permute-start
  356.1 225.8 %reduce-scatter.11.cloned.1.call-start = ((), (), s32[]{:S(2)}) async-start(), calls=%async_computation.13 | async-start | bytes 4456448 | tf_op jit(solution)/shard_map/reduce_scatter | solution.py:414
  363.9 2.4 collective-permute-start.6
  364.3 1.9 collective-permute-start.7
  369.6 310.0 %reduce-scatter.9.cloned.1.call-start = ((), (), s32[]{:S(2)}) async-start(), calls=%async_computation.11 | async-start | bytes 4456448 | tf_op jit(solution)/shard_map/reduce_scatter | solution.py:414
  369.6 3.1 collective-permute-start.5
  370.9 1.6 collective-permute-start.4
  377.5 382.4 %reduce-scatter.7.cloned.1.call-start = ((), (), s32[]{:S(2)}) async-start(), calls=%async_computation.10 | async-start | bytes 1114112 | tf_op jit(solution)/shard_map/reduce_scatter | solution.py:414
  378.5 1.8 collective-permute-start.3
  378.9 1.4 collective-permute-start.2
  381.8 405.4 %all-gather.13.cloned.1.call-start = ((), (), s32[]{:S(2)}) async-start(), calls=%async_computation.9 | async-start | bytes 1769472 | tf_op jit(solution)/shard_map/all_gather | solution.py:415
  484.9 331.7 %all-gather.17.cloned.1.call-start = ((), (), s32[]{:S(2)}) async-start(), calls=%async_computation.14 | async-start | bytes 2359296 | tf_op jit(solution)/shard_map/all_gather | solution.py:415
  582.0 264.6 %all-gather.15.cloned.1.call-start = ((), (), s32[]{:S(2)}) async-start(), calls=%async_computation.12 | async-start | bytes 2359296 | tf_op jit(solution)/shard_map/all_gather | solution.py:415
  679.5 46.3 %copy-start.7 = (f32[128,1024]{1,0:T(8,128)S(1)}, f32[128,1024]{1,0:T(8,128)}, u32[]{:S(2)}) copy-start(f32[128,1024]{1,0:T(8,128)} %copy-done.6) | copy-start | bytes 1572868
  816.6 34.1 %copy-start.1 = (bf16[1,256,4096]{2,1,0:T(8,128)(2,1)S(1)}, bf16[1,256,4096]{2,1,0:T(8,128)(2,1)}, u32[]{:S(2)}) copy-start(bf16[1,256,4096]{2,1,0:T(8,128)(2,1)} %param.28) | copy-start | bytes 6291460
  (14 other events, 46.6 us)
Sparse Core Ops, SparseCore 0:
  11.6 72.2 all-gather.18
  87.3 55.2 all-gather.20
  146.0 76.2 all-gather.22
  225.6 75.9 all-gather.24
  356.3 128.5 reduce-scatter.4
  487.6 94.3 reduce-scatter.10
  584.8 94.6 reduce-scatter.8
  682.3 77.5 reduce-scatter.6
  762.0 24.6 all-gather.12
  788.6 27.9 all-gather.16
  818.6 27.8 all-gather.14

commit v2 on v1

--- a/solution.py
+++ b/solution.py
@@ -164,6 +164,56 @@
 
 def swap_cores(rows):
     return lax.ppermute(rows, "core", [(0, 1), (1, 0)])
+
+
+def swap_bit(rows, axis, bit):
+    count = lax.axis_size(axis)
+    return lax.ppermute(rows, axis, [(i, i ^ (1 << bit)) for i in range(count)])
+
+
+def bits_of(axis):
+    return lax.axis_size(axis).bit_length() - 1
+
+
+def bit_order(reverse):
+    order = list(range(bits_of("chip")))
+    return order[::-1] if reverse else order
+
+
+def halve(block, axis, order):
+    count = bits_of(axis)
+    block = block.reshape((2,) * count + block.shape[1:])
+    left = list(range(count))[::-1]
+    me = lax.axis_index(axis)
+    for bit in order:
+        place = left.index(bit)
+        left.pop(place)
+        mine = (me >> bit) & 1
+        kept = lax.dynamic_index_in_dim(block, mine, place, keepdims=False)
+        sent = lax.dynamic_index_in_dim(block, 1 - mine, place, keepdims=False)
+        got = swap_bit(sent, axis, bit)
+        block = (kept.astype(jnp.float32) + got.astype(jnp.float32)).astype(block.dtype)
+    return block
+
+
+def double(block, axis, order):
+    me = lax.axis_index(axis)
+    seen = []
+    for bit in order:
+        got = swap_bit(block, axis, bit)
+        low = ((me >> bit) & 1) == 0
+        block = jnp.stack([jnp.where(low, block, got), jnp.where(low, got, block)])
+        seen.insert(0, bit)
+    count = len(order)
+    want = list(range(count))[::-1]
+    block = block.transpose([seen.index(bit) for bit in want] + list(range(count, block.ndim)))
+    return block.reshape((2**count,) + block.shape[count:])
+
+
+def total_over(block, axis):
+    for bit in range(bits_of(axis)):
+        block = block + swap_bit(block, axis, bit)
+    return block
 
 
 def to_heads(rows, parts):
@@ -377,7 +427,8 @@
         ln1_gain, ln1_bias, query_bias, value_bias, proj_bias, ln2_gain, ln2_bias, fc_bias, out_bias,
     )
     sizes = [v.shape[1] for v in vectors_in]
-    gathered = lax.all_gather(jnp.concatenate([v[0] for v in vectors_in]), "fsdp", axis=0)
+    gathered = double(jnp.concatenate([v[0] for v in vectors_in])[None], "fsdp", list(range(bits_of("fsdp"))))
+    gathered = gathered.reshape(groups, -1)
     gathered_vectors = []
     start = 0
     for size in sizes:
@@ -385,38 +436,58 @@
         start += size
     me = lax.axis_index(CTX)
 
-    def gather_weight(weight):
+    def own_piece(weight):
         rows = weight.shape[1] // contexts
-        piece = lax.dynamic_slice_in_dim(weight[0], me * rows, rows, axis=0)
-        return lax.all_gather(piece, ("fsdp",) + CTX, axis=0, tiled=True)
-
-    qkv_full = gather_weight(qkv_weight)
-    proj_full = gather_weight(proj_weight)
-    fc_full = gather_weight(fc_weight)
-    out_full = gather_weight(out_weight)
+        return lax.dynamic_slice_in_dim(weight[0], me * rows, rows, axis=0)
+
+    def gather_joined(pieces):
+        return lax.all_gather(jnp.concatenate(pieces, axis=1), ("fsdp",) + CTX, axis=0, tiled=True)
+
+    first = gather_joined((own_piece(qkv_weight), own_piece(proj_weight)))
+    qkv_full, proj_full = first[:, : 3 * D], first[:, 3 * D :]
+    fc_piece, out_piece = own_piece(fc_weight), own_piece(out_weight)
+    rows = fc_piece.shape[0]
+    quarters = out_piece.shape[0] // rows
+    second = gather_joined(
+        (fc_piece,) + tuple(out_piece[q * rows : (q + 1) * rows] for q in range(quarters))
+    )
+    hidden = fc_piece.shape[1]
+    fc_full = second[:, :hidden]
+    out_full = second[:, hidden:].reshape(groups * contexts, rows, quarters, D)
+    out_full = out_full.transpose(0, 2, 1, 3).reshape(groups * contexts * rows * quarters, D)
     g = gathered_vectors
     full_weights = (
         g[0], g[1], qkv_full, g[2], g[3], proj_full, g[4], g[5], g[6], fc_full, g[7], out_full, g[8],
     )
     stream, record = layer_forward(stream, full_weights, position)
     upstream, vectors, row_pairs = layer_backward(cotangent[0], full_weights, record, position)
-    matrices = []
-    for left, right in row_pairs:
+    z_bits = list(range(bits_of("fsdp")))
+    chips = lax.axis_size("chip")
+    core = lax.axis_index("core")
+    matrices = [None] * 4
+    for index in (3, 2, 1, 0):
+        left, right = row_pairs[index]
         features = left.shape[1] // (groups * 2)
         pieces = left.reshape(row_count, groups, 2, features)
         pieces = pieces.transpose(2, 0, 1, 3).reshape(2, row_count, groups * features)
-        core = lax.axis_index("core")
         own_half = lax.dynamic_index_in_dim(pieces, core, 0, keepdims=False)
         sent_half = lax.dynamic_index_in_dim(pieces, 1 - core, 0, keepdims=False)
         left_half = jnp.concatenate([own_half, swap_cores(sent_half)])
         right_pair = jnp.concatenate([right, swap_cores(right)])
-        terms = dot_tn(left_half, right_pair).astype(jnp.bfloat16)
-        part = lax.psum_scatter(terms, ("fsdp", "chip"), scatter_dimension=0, tiled=True)
-        total = lax.all_gather(part, ("core", "chip"), axis=0, tiled=True)
-        matrices.append(total.astype(jnp.float32)[None])
+        width = right.shape[1] // 2
+        done = []
+        for side in range(2):
+            order = bit_order(side == 1)
+            terms = dot_tn(left_half, right_pair[:, side * width : (side + 1) * width])
+            terms = terms.astype(jnp.bfloat16).reshape(groups, chips, features // chips, width)
+            terms = halve(terms.transpose(1, 0, 2, 3), "chip", order)
+            part = halve(terms, "fsdp", z_bits[::-1])
+            part = double(double(part, "chip", order), "core", [0])
+            done.append(part.reshape(2 * features, width).astype(jnp.float32))
+        matrices[index] = jnp.concatenate(done, axis=1)[None]
     packed = jnp.concatenate([v.reshape(groups, -1) for v in vectors], axis=1)
-    summed = lax.psum(packed, ("fsdp",) + CTX)
-    own = lax.dynamic_index_in_dim(summed, lax.axis_index("fsdp"), 0, keepdims=True)
+    packed = halve(packed, "fsdp", z_bits[::-1])
+    own = total_over(total_over(packed, "core"), "chip")[None]
     vector_parts = []
     start = 0
     for v in vectors:

time: 858 us -> 596 us (0.69)
  waiting for transfers between devices: 622 us -> 331 us
  blocking collectives: 105 us -> 0 us
  starting transfers between devices: 10.2 us -> 80.4 us
  local copies, waits for them, and re-layouts: 24.9 us -> 75.3 us
    reduce_scatter x4 -> x0, waiting for transfers between devices: 325 us -> none  [shards(): lax.psum_scatter(terms, ('fsdp', 'chip'), scatter_dimension=0, tiled=True)]
    ppermute x0 -> x63, waiting for transfers between devices: none -> 173 us  [swap_bit(): return lax.ppermute(rows, axis, [(i, i ^ 1 << bit) for i in range(count)])]
    all_gather x7 -> x2, waiting for transfers between devices: 279 us -> 136 us  [gather_joined(): lax.all_gather(jnp.concatenate(pieces, axis=1), ('fsdp',) + CTX, axis=0,...]
    ppermute x0 -> x63, starting transfers between devices: none -> 63.3 us  [swap_bit(): return lax.ppermute(rows, axis, [(i, i ^ 1 << bit) for i in range(count)])]
    all_gather x2 -> x0, blocking collectives: 40.9 us -> none  [the longest x1 26.1 us: shards(): total = lax.all_gather(part, ('core', 'chip'), axis=0, tiled=True)]
    psum x1 -> x0, blocking collectives: 39.6 us -> none  [shards(): summed = lax.psum(packed, ('fsdp',) + CTX)]
    all_to_all x2 -> x0, blocking collectives: 24.5 us -> none  [the longest x1 15 us: to_tokens(): moved = lax.all_to_all(joined, CTX, split_axis=0, concat_axis=0, tiled=True)]
    reshape x7 -> x1, local copies, waits for them, and re-layouts: 0.07 us -> 14.5 us  [shards(): out_full = second[:, hidden:].reshape(groups * contexts, rows, quarters, D)]
  transfers between devices with their start and end apart: 21 -> 77, of which waited for: 16 -> 40; matrix products, arithmetic and copies ran while one was open for 8% -> 23% of each run, Pallas kernels for 1% -> 2%
where the time goes in v2:
time: 596 us; the launch traced here: 588 us
  waiting for transfers between devices  331 us (56%)
  starting transfers between devices  80.4 us (13%)
  local copies, waits for them, and re-layouts  75.3 us (13%)
  matrix products  49.5 us (8%)
  other arithmetic  20.7 us (3%)
  between operations  16.6 us (3%)
  Pallas kernels  14.7 us (2%)
    ppermute x63, waiting for transfers between devices, swap_bit(): return lax.ppermute(rows, axis, [(i, i ^ 1 << bit) for i in range(count)])  173 us
    all_gather x2, waiting for transfers between devices, gather_joined(): lax.all_gather(jnp.concatenate(pieces, axis=1), ('fsdp',) + CTX, axis=0,...  136 us
    ppermute x63, starting transfers between devices, swap_bit(): return lax.ppermute(rows, axis, [(i, i ^ 1 << bit) for i in range(count)])  63.3 us
    reshape x1, local copies, waits for them, and re-layouts, shards(): out_full = second[:, hidden:].reshape(groups * contexts, rows, quarters, D)  14.5 us
    all_to_all x2, waiting for transfers between devices, to_heads(): lax.all_to_all(stacked, CTX, split_axis=0, concat_axis=0, tiled=True)  13.8 us
    dot_general x8, matrix products, dot_tn(): lax.dot_general(left, right, (((0,), (0,)), ((), ())), preferred_element_...  12.7 us
  transfers between devices with their start and end apart: 77, of which 40 were waited for; matrix products, arithmetic and copies ran while one was open for 23% of the time, Pallas kernels for 2%

profile of v2, /device:TPU:0, one launch (start us, length us, event | category | flops | bytes accessed | tf_op | source)
XLA Modules:
  0.0 588.2 jit_solution(16558314761034630410)
XLA Ops:
  26.7 65.1 %all-gather.3.cloned.1.call-done = bf16[1024,4096]{1,0:T(8,128)(2,1)} async-done(((bf16[32,4096]{1,0:T(8,128)(2,1)}), bf16[1024,4096]{1,0:T(8,128)(2,1)}) %all-gather.3.cloned.1.call-update) | async-done | bytes 8388624 | tf_op jit(solution)/shard_map/all_gather | solution.py:444
  91.8 3.9 fusion.36
  103.2 13.8 %all-to-all-done = bf16[8,128,384]{1,2,0:T(8,128)(2,1)S(1)} async-done(((bf16[8,128,384]{1,2,0:T(8,128)(2,1)}), bf16[8,128,384]{1,2,0:T(8,128)(2,1)S(1)}, u32[]{:S(2)}, u32[]{:S(2)}) %all-to-all-start) | async-done | bytes 786464 | tf_op jit(solution)/shard_map/all_to_all | solution.py:224
  117.6 5.6 shard_map.271
  124.0 3.9 all-to-all-start.1
  129.1 8.5 %all-to-all-done.1 = bf16[8,128,128]{1,2,0:T(8,128)(2,1)S(1)} async-done(((bf16[8,128,128]{1,2,0:T(8,128)(2,1)}), bf16[8,128,128]{1,2,0:T(8,128)(2,1)S(1)}, u32[]{:S(2)}, u32[]{:S(2)}) %all-to-all-start.1) | async-done | bytes 262176 | tf_op jit(solution)/shard_map/all_to_all | solution.py:235
  145.8 70.5 %all-gather.5.cloned.1.call-done = bf16[1024,8192]{1,0:T(8,128)(2,1)} async-done(((bf16[32,8192]{1,0:T(8,128)(2,1)}), bf16[1024,8192]{1,0:T(8,128)(2,1)}) %all-gather.5.cloned.1.call-update) | async-done | bytes 16777232 | tf_op jit(solution)/shard_map/all_gather | solution.py:444
  216.3 7.8 %slice.186 = bf16[1024,4096]{1,0:T(8,128)(2,1)} slice(bf16[1024,8192]{1,0:T(8,128)(2,1)} %all-gather.5.cloned.1.call-done), slice={[0:1024], [4096:8192]} | slice | bytes 16777216 | tf_op jit(solution)/shard_map/slice | solution.py:456
  224.1 14.5 %reshape.518 = bf16[32,32,4,1024]{3,2,1,0:T(4,128)(2,1)} reshape(bf16[1024,4096]{1,0:T(8,128)(2,1)} %slice.186) | data formatting | bytes 16777216 | tf_op jit(solution)/shard_map/reshape | solution.py:456
  238.6 10.4 %copy.61 = bf16[32,4,32,1024]{3,2,1,0:T(8,128)(2,1)} copy(bf16[32,4,32,1024]{3,1,2,0:T(4,128)(2,1)} %bitcast.555) | data formatting | bytes 16777216 | tf_op jit(solution)/shard_map/transpose | solution.py:457
  249.0 6.9 %multiply_convert_fusion = (bf16[128,4096]{1,0:T(8,128)(2,1)}, f32[128,4096]{1,0:T(8,128)}) fusion(f32[4096]{0:T(1024)S(1)} %bitcast.633, bf16[128,1024]{1,0:T(8,128)(2,1)S(1)} %add_convert_fusion.1, bf16[1024,8192]{1,0:T(8,128)(2,1)} %all-gather.5.cloned.1.call-done), kind=kOutput, calls=%fused_computation.40 | convolution fusion | flops 1078984704 | bytes 11812864 | tf_op jit(solution)/shard_map/dot_general | solution.py:274
  258.7 5.9 %fusion.46 = f32[1,128,1024]{2,1,0:T(8,128)} fusion(f32[128,1024]{1,0:T(8,128)S(1)} %get-tuple-element.129, bf16[128,4096]{1,0:T(8,128)(2,1)} %get-tuple-element.130, bf16[4096,1024]{1,0:T(8,128)(2,1)} %bitcast.553, f32[1024]{0:T(1024)S(1)} %bitcast.630), kind=kOutput, calls=%fused_computation.60 | convolution fusion | flops 1074003968 | bytes 10489856 | tf_op jit(solution)/shard_map/dot_general | solution.py:279
  264.6 7.1 %fusion.116 = (f32[4096]{0:T(1024)S(1)}, bf16[128,4096]{1,0:T(8,128)(2,1)S(1)}) fusion(f32[128,4096]{1,0:T(8,128)S(1)} %copy-done.43, bf16[4096,1024]{1,0:T(8,128)(2,1)} %bitcast.554, f32[1,128,1024]{2,1,0:T(8,128)S(1)} %copy-done.12), kind=kOutput, calls=%fused_computation.345 | convolution fusion | flops 1084354560 | bytes 12075008 | tf_op jit(solution)/shard_map/dot_general | solution.py:335
  290.6 9.1 %shard_map.272 = (f32[1024,128]{1,0:T(8,128)S(1)}, f32[1024,128]{1,0:T(8,128)S(1)}, f32[1024,128]{1,0:T(8,128)S(1)}) custom-call(bf16[1024,128]{1,0:T(8,128)(2,1)S(1)} %get-tuple-element.55.q_ref, bf16[1024,128]{1,0:T(8,128)(2,1)S(1)} %get-tuple-element.54.k_ref, bf16[1024,128]{1,0:T(8,128)(2,1)S(1)} %get-tuple-element.53.v_ref, ...), custom_call_target="tpu_custom_call" | custom-call | flops 1342177280 | bytes 2883584 | tf_op jit(solution)/shard_map/pallas_call | solution.py:152
  301.2 4.3 all-to-all-start.3
  316.5 6.2 %collective-permute-done.32 = bf16[2,4,32,512]{3,2,0,1:T(8,128)(2,1)} collective-permute-done((bf16[2,4,32,512]{3,2,0,1:T(8,128)(2,1)}, bf16[2,4,32,512]{3,2,0,1:T(8,128)(2,1)}, u32[]{:S(2)}, u32[]{:S(2)}) %collective-permute-start.32) | collective-permute-done | bytes 262176 | tf_op jit(solution)/shard_map/ppermute | solution.py:171
  336.2 4.8 collective-permute-done.34
  355.4 5.4 multiply_reduce_fusion.1
  361.8 4.1 collective-permute-done.2
  379.1 20.0 %collective-permute-done.6 = f32[3072]{0:T(1024)S(1)} collective-permute-done((f32[3072]{0:T(1024)S(1)}, f32[3072]{0:T(1024)S(1)}, u32[]{:S(2)}, u32[]{:S(2)}) %collective-permute-start.6) | collective-permute-done | bytes 12320 | tf_op jit(solution)/shard_map/ppermute | solution.py:171
  408.5 16.8 %collective-permute-done.57 = bf16[2,4,128,512]{3,2,0,1:T(8,128)(2,1)S(1)} collective-permute-done((bf16[2,4,128,512]{3,2,0,1:T(8,128)(2,1)S(1)}, bf16[2,4,128,512]{3,2,0,1:T(8,128)(2,1)S(1)}, u32[]{:S(2)}, u32[]{:S(2)}) %collective-permute-start.57) | collective-permute-done | bytes 1048608 | tf_op jit(solution)/shard_map/ppermute | solution.py:171
  433.6 14.2 %collective-permute-done.41 = bf16[2,4,32,2048]{3,2,0,1:T(8,128)(2,1)S(1)} collective-permute-done((bf16[2,4,32,2048]{3,2,0,1:T(8,128)(2,1)S(1)}, bf16[2,4,32,2048]{3,2,0,1:T(8,128)(2,1)S(1)}, u32[]{:S(2)}, u32[]{:S(2)}) %collective-permute-start.41) | collective-permute-done | bytes 1048608 | tf_op jit(solution)/shard_map/ppermute | solution.py:171
  448.8 10.2 %collective-permute-done.65 = bf16[4,128,512]{2,1,0:T(8,128)(2,1)S(1)} collective-permute-done((bf16[4,128,512]{2,1,0:T(8,128)(2,1)S(1)}, bf16[4,128,512]{2,1,0:T(8,128)(2,1)S(1)}, u32[]{:S(2)}, u32[]{:S(2)}) %collective-permute-start.65) | collective-permute-done | bytes 524320 | tf_op jit(solution)/shard_map/ppermute | solution.py:171
  461.9 12.8 %collective-permute-done.66 = bf16[2,128,512]{2,1,0:T(8,128)(2,1)S(1)} collective-permute-done((bf16[2,128,512]{2,1,0:T(8,128)(2,1)S(1)}, bf16[2,128,512]{2,1,0:T(8,128)(2,1)S(1)}, u32[]{:S(2)}, u32[]{:S(2)}) %collective-permute-start.66) | collective-permute-done | bytes 262176 | tf_op jit(solution)/shard_map/ppermute | solution.py:171
  474.8 9.3 %collective-permute-done.59 = bf16[2,128,512]{2,1,0:T(8,128)(2,1)S(1)} collective-permute-done((bf16[2,128,512]{2,1,0:T(8,128)(2,1)S(1)}, bf16[2,128,512]{2,1,0:T(8,128)(2,1)S(1)}, u32[]{:S(2)}, u32[]{:S(2)}) %collective-permute-start.59) | collective-permute-done | bytes 262176 | tf_op jit(solution)/shard_map/ppermute | solution.py:171
  492.7 8.1 %collective-permute-done.68 = bf16[128,512]{1,0:T(8,128)(2,1)S(1)} collective-permute-done((bf16[128,512]{1,0:T(8,128)(2,1)S(1)}, bf16[128,512]{1,0:T(8,128)(2,1)S(1)}, u32[]{:S(2)}, u32[]{:S(2)}) %collective-permute-start.68) | collective-permute-done | bytes 131104 | tf_op jit(solution)/shard_map/ppermute | solution.py:171
  515.6 12.4 %collective-permute-done.50 = bf16[2,32,2048]{2,1,0:T(8,128)(2,1)S(1)} collective-permute-done((bf16[2,32,2048]{2,1,0:T(8,128)(2,1)S(1)}, bf16[2,32,2048]{2,1,0:T(8,128)(2,1)S(1)}, u32[]{:S(2)}, u32[]{:S(2)}) %collective-permute-start.50) | collective-permute-done | bytes 262176 | tf_op jit(solution)/shard_map/ppermute | solution.py:171
  528.1 5.0 collective-permute-done.43
  533.2 6.8 %collective-permute-done.51 = bf16[32,2048]{1,0:T(8,128)(2,1)S(1)} collective-permute-done((bf16[32,2048]{1,0:T(8,128)(2,1)S(1)}, bf16[32,2048]{1,0:T(8,128)(2,1)S(1)}, u32[]{:S(2)}, u32[]{:S(2)}) %collective-permute-start.51) | collective-permute-done | bytes 131104 | tf_op jit(solution)/shard_map/ppermute | solution.py:171
  540.0 5.4 collective-permute-done.44
  556.7 5.3 collective-permute-done.20
  562.4 5.2 collective-permute-done.13
  (478 shorter events, 182.4 us)
Async XLA Ops:
  7.3 84.5 %all-gather.3.cloned.1.call-start = ((), (), s32[]{:S(2)}) async-start(), calls=%async_computation.4 | async-start | bytes 8650752 | tf_op jit(solution)/shard_map/all_gather | solution.py:444
  9.4 206.9 %all-gather.5.cloned.1.call-start = ((), (), s32[]{:S(2)}) async-start(), calls=%async_computation.5 | async-start | bytes 17301504 | tf_op jit(solution)/shard_map/all_gather | solution.py:444
  20.6 304.8 %collective-permute-start.56 = (bf16[128,1024]{1,0:T(8,128)(2,1)}, bf16[128,1024]{1,0:T(8,128)(2,1)}, u32[]{:S(2)}, u32[]{:S(2)}) collective-permute-start(bf16[128,1024]{1,0:T(8,128)(2,1)} %get-tuple-element.60), channel_id=1, source_target_pairs={{0,4},{4,0},{1,5},{5,1},{2,6},{6,2},{3,7},{7,3},{8,12},{12,8},{9,1... | collective-permute-start | bytes 786440 | tf_op jit(solution)/shard_map/ppermute | solution.py:166
  97.2 19.8 %all-to-all-start = ((bf16[8,128,384]{1,2,0:T(8,128)(2,1)}), bf16[8,128,384]{1,2,0:T(8,128)(2,1)S(1)}, u32[]{:S(2)}, u32[]{:S(2)}) async-start(bf16[8,128,384]{1,2,0:T(8,128)(2,1)} %bitcast.8), calls=%async_computation | async-start | bytes 1572864 | tf_op jit(solution)/shard_map/all_to_all | solution.py:224
  128.7 297.5 %collective-permute-start.7 = (bf16[128,512]{0,1:T(8,128)(2,1)}, bf16[128,512]{0,1:T(8,128)(2,1)}, u32[]{:S(2)}, u32[]{:S(2)}) collective-permute-start(bf16[128,512]{0,1:T(8,128)(2,1)} %get-tuple-element.91), channel_id=1, source_target_pairs={{0,4},{4,0},{1,5},{5,1},{2,6},{6,2},{3,7},{7,3},{8,12},{12,8},{9,1... | collective-permute-start | bytes 393224 | tf_op jit(solution)/shard_map/ppermute | solution.py:166
  138.4 167.1 %collective-permute-start.23 = (bf16[128,512]{0,1:T(8,128)(2,1)}, bf16[128,512]{0,1:T(8,128)(2,1)}, u32[]{:S(2)}, u32[]{:S(2)}) collective-permute-start(bf16[128,512]{0,1:T(8,128)(2,1)} %get-tuple-element.89), channel_id=1, source_target_pairs={{0,4},{4,0},{1,5},{5,1},{2,6},{6,2},{3,7},{7,3},{8,12},{12,8},{9,1... | collective-permute-start | bytes 393224 | tf_op jit(solution)/shard_map/ppermute | solution.py:166
  145.3 255.6 %collective-permute-start.39 = (bf16[128,512]{0,1:T(8,128)(2,1)}, bf16[128,512]{0,1:T(8,128)(2,1)}, u32[]{:S(2)}, u32[]{:S(2)}) collective-permute-start(bf16[128,512]{0,1:T(8,128)(2,1)} %get-tuple-element.83), channel_id=1, source_target_pairs={{0,4},{4,0},{1,5},{5,1},{2,6},{6,2},{3,7},{7,3},{8,12},{12,8},{9,1... | collective-permute-start | bytes 393224 | tf_op jit(solution)/shard_map/ppermute | solution.py:166
  275.9 29.6 %collective-permute-start.24 = (bf16[128,1024]{1,0:T(8,128)(2,1)S(1)}, bf16[128,1024]{1,0:T(8,128)(2,1)}, u32[]{:S(2)}, u32[]{:S(2)}) collective-permute-start(bf16[128,1024]{1,0:T(8,128)(2,1)S(1)} %convert_element_type.608), channel_id=1, source_target_pairs={{0,4},{4,0},{1,5},{5,1},{2,6},{6,2},{3,7},{7,3},{8,12},{12,8},{9,1... | collective-permute-start | bytes 786440 | tf_op jit(solution)/shard_map/ppermute | solution.py:166
  301.2 54.1 %all-to-all-start.3 = ((bf16[8,128,384]{1,2,0:T(8,128)(2,1)}), bf16[8,128,384]{1,2,0:T(8,128)(2,1)S(1)}, u32[]{:S(2)}, u32[]{:S(2)}) async-start(bf16[8,128,384]{1,2,0:T(8,128)(2,1)} %copy.64), calls=%async_computation.3 | async-start | bytes 1572864 | tf_op jit(solution)/shard_map/all_to_all | solution.py:235
  323.7 77.3 %collective-permute-start.40 = (bf16[128,4096]{1,0:T(8,128)(2,1)S(1)}, bf16[128,4096]{1,0:T(8,128)(2,1)}, u32[]{:S(2)}, u32[]{:S(2)}) collective-permute-start(bf16[128,4096]{1,0:T(8,128)(2,1)S(1)} %copy-done.8), channel_id=1, source_target_pairs={{0,4},{4,0},{1,5},{5,1},{2,6},{6,2},{3,7},{7,3},{8,12},{12,8},{9,1... | collective-permute-start | bytes 3145736 | tf_op jit(solution)/shard_map/ppermute | solution.py:166
  353.5 21.7 %collective-permute-start.38 = (bf16[4,32,512]{2,1,0:T(8,128)(2,1)S(1)}, bf16[4,32,512]{2,1,0:T(8,128)(2,1)S(1)}, u32[]{:S(2)}, u32[]{:S(2)}) collective-permute-start(bf16[4,32,512]{2,1,0:T(8,128)(2,1)S(1)} %bitcast.613), channel_id=1, source_target_pairs={{0,4},{4,0},{1,5},{5,1},{2,6},{6,2},{3,7},{7,3},{8,12},{12,8},{9,1... | collective-permute-start | bytes 393224 | tf_op jit(solution)/shard_map/ppermute | solution.py:171
  374.6 32.0 %collective-permute-start.64 = (bf16[2,4,128,512]{3,2,0,1:T(8,128)(2,1)}, bf16[2,4,128,512]{3,2,0,1:T(8,128)(2,1)S(1)}, u32[]{:S(2)}, u32[]{:S(2)}) collective-permute-start(bf16[2,4,128,512]{3,2,0,1:T(8,128)(2,1)} %dynamic-slice_bitcast_fusion), channel_id=1, source_target_pairs={{0,16},{8,24},{16,0},{24,8},{1,17},{9,25},{17,1},{25,9},{2,18},{10... | collective-permute-start | bytes 3145736 | tf_op jit(solution)/shard_map/ppermute | solution.py:171
  376.5 22.7 %collective-permute-start.6 = (f32[3072]{0:T(1024)S(1)}, f32[3072]{0:T(1024)S(1)}, u32[]{:S(2)}, u32[]{:S(2)}) collective-permute-start(f32[3072]{0:T(1024)S(1)} %add.412), channel_id=1, source_target_pairs={{0,16},{8,24},{16,0},{24,8},{1,17},{9,25},{17,1},{25,9},{2,18},{10... | collective-permute-start | bytes 36872 | tf_op jit(solution)/shard_map/ppermute | solution.py:171
  399.2 26.1 %collective-permute-start.57 = (bf16[2,4,128,512]{3,2,0,1:T(8,128)(2,1)S(1)}, bf16[2,4,128,512]{3,2,0,1:T(8,128)(2,1)S(1)}, u32[]{:S(2)}, u32[]{:S(2)}) collective-permute-start(bf16[2,4,128,512]{3,2,0,1:T(8,128)(2,1)S(1)} %copy-done.17), channel_id=1, source_target_pairs={{0,8},{8,0},{16,24},{24,16},{1,9},{9,1},{17,25},{25,17},{2,10},{10... | collective-permute-start | bytes 3145736 | tf_op jit(solution)/shard_map/ppermute | solution.py:171
  401.0 27.0 %collective-permute-start.8 = (bf16[128,3072]{0,1:T(8,128)(2,1)S(1)}, bf16[128,3072]{0,1:T(8,128)(2,1)S(1)}, u32[]{:S(2)}, u32[]{:S(2)}) collective-permute-start(bf16[128,3072]{0,1:T(8,128)(2,1)S(1)} %bitcast.578), channel_id=1, source_target_pairs={{0,4},{4,0},{1,5},{5,1},{2,6},{6,2},{3,7},{7,3},{8,12},{12,8},{9,1... | collective-permute-start | bytes 2359304 | tf_op jit(solution)/shard_map/ppermute | solution.py:166
  403.0 28.6 %collective-permute-start.48 = (bf16[2,4,32,2048]{3,2,0,1:T(8,128)(2,1)S(1)}, bf16[2,4,32,2048]{3,2,0,1:T(8,128)(2,1)S(1)}, u32[]{:S(2)}, u32[]{:S(2)}) collective-permute-start(bf16[2,4,32,2048]{3,2,0,1:T(8,128)(2,1)S(1)} %dynamic-slice_bitcast_fusion.2), channel_id=1, source_target_pairs={{0,16},{8,24},{16,0},{24,8},{1,17},{9,25},{17,1},{25,9},{2,18},{10... | collective-permute-start | bytes 3145736 | tf_op jit(solution)/shard_map/ppermute | solution.py:171
  406.7 41.1 %collective-permute-start.41 = (bf16[2,4,32,2048]{3,2,0,1:T(8,128)(2,1)S(1)}, bf16[2,4,32,2048]{3,2,0,1:T(8,128)(2,1)S(1)}, u32[]{:S(2)}, u32[]{:S(2)}) collective-permute-start(bf16[2,4,32,2048]{3,2,0,1:T(8,128)(2,1)S(1)} %dynamic-slice_bitcast_fusion.3), channel_id=1, source_target_pairs={{0,8},{8,0},{16,24},{24,16},{1,9},{9,1},{17,25},{25,17},{2,10},{10... | collective-permute-start | bytes 3145736 | tf_op jit(solution)/shard_map/ppermute | solution.py:171
  425.3 33.7 %collective-permute-start.65 = (bf16[4,128,512]{2,1,0:T(8,128)(2,1)S(1)}, bf16[4,128,512]{2,1,0:T(8,128)(2,1)S(1)}, u32[]{:S(2)}, u32[]{:S(2)}) collective-permute-start(bf16[4,128,512]{2,1,0:T(8,128)(2,1)S(1)} %dynamic-slice_bitcast_fusion.6), channel_id=1, source_target_pairs={{0,8},{8,0},{16,24},{24,16},{1,9},{9,1},{17,25},{25,17},{2,10},{10... | collective-permute-start | bytes 1572872 | tf_op jit(solution)/shard_map/ppermute | solution.py:171
  426.3 33.7 %collective-permute-start.58 = (bf16[4,128,512]{2,1,0:T(8,128)(2,1)S(1)}, bf16[4,128,512]{2,1,0:T(8,128)(2,1)S(1)}, u32[]{:S(2)}, u32[]{:S(2)}) collective-permute-start(bf16[4,128,512]{2,1,0:T(8,128)(2,1)S(1)} %dynamic-slice_bitcast_fusion.7), channel_id=1, source_target_pairs={{0,16},{8,24},{16,0},{24,8},{1,17},{9,25},{17,1},{25,9},{2,18},{10... | collective-permute-start | bytes 1572872 | tf_op jit(solution)/shard_map/ppermute | solution.py:171
  429.5 54.7 %collective-permute-start.16 = (bf16[2,4,32,1536]{3,2,0,1:T(8,128)(2,1)S(1)}, bf16[2,4,32,1536]{3,2,0,1:T(8,128)(2,1)S(1)}, u32[]{:S(2)}, u32[]{:S(2)}) collective-permute-start(bf16[2,4,32,1536]{3,2,0,1:T(8,128)(2,1)S(1)} %dynamic-slice_bitcast_fusion.4), channel_id=1, source_target_pairs={{0,16},{8,24},{16,0},{24,8},{1,17},{9,25},{17,1},{25,9},{2,18},{10... | collective-permute-start | bytes 2359304 | tf_op jit(solution)/shard_map/ppermute | solution.py:171
  431.6 55.0 %collective-permute-start.9 = (bf16[2,4,32,1536]{3,2,0,1:T(8,128)(2,1)S(1)}, bf16[2,4,32,1536]{3,2,0,1:T(8,128)(2,1)S(1)}, u32[]{:S(2)}, u32[]{:S(2)}) collective-permute-start(bf16[2,4,32,1536]{3,2,0,1:T(8,128)(2,1)S(1)} %dynamic-slice_bitcast_fusion.5), channel_id=1, source_target_pairs={{0,8},{8,0},{16,24},{24,16},{1,9},{9,1},{17,25},{25,17},{2,10},{10... | collective-permute-start | bytes 2359304 | tf_op jit(solution)/shard_map/ppermute | solution.py:171
  447.7 60.2 %collective-permute-start.49 = (bf16[4,32,2048]{2,1,0:T(8,128)(2,1)S(1)}, bf16[4,32,2048]{2,1,0:T(8,128)(2,1)S(1)}, u32[]{:S(2)}, u32[]{:S(2)}) collective-permute-start(bf16[4,32,2048]{2,1,0:T(8,128)(2,1)S(1)} %dynamic-slice_bitcast_fusion.10), channel_id=1, source_target_pairs={{0,8},{8,0},{16,24},{24,16},{1,9},{9,1},{17,25},{25,17},{2,10},{10... | collective-permute-start | bytes 1572872 | tf_op jit(solution)/shard_map/ppermute | solution.py:171
  459.0 49.8 %collective-permute-start.42 = (bf16[4,32,2048]{2,1,0:T(8,128)(2,1)S(1)}, bf16[4,32,2048]{2,1,0:T(8,128)(2,1)S(1)}, u32[]{:S(2)}, u32[]{:S(2)}) collective-permute-start(bf16[4,32,2048]{2,1,0:T(8,128)(2,1)S(1)} %dynamic-slice_bitcast_fusion.11), channel_id=1, source_target_pairs={{0,16},{8,24},{16,0},{24,8},{1,17},{9,25},{17,1},{25,9},{2,18},{10... | collective-permute-start | bytes 1572872 | tf_op jit(solution)/shard_map/ppermute | solution.py:171
  486.6 22.5 %collective-permute-start.17 = (bf16[4,32,1536]{2,1,0:T(8,128)(2,1)S(1)}, bf16[4,32,1536]{2,1,0:T(8,128)(2,1)S(1)}, u32[]{:S(2)}, u32[]{:S(2)}) collective-permute-start(bf16[4,32,1536]{2,1,0:T(8,128)(2,1)S(1)} %dynamic-slice_bitcast_fusion.12), channel_id=1, source_target_pairs={{0,8},{8,0},{16,24},{24,16},{1,9},{9,1},{17,25},{25,17},{2,10},{10... | collective-permute-start | bytes 1179656 | tf_op jit(solution)/shard_map/ppermute | solution.py:171
  489.3 22.8 %collective-permute-start.10 = (bf16[4,32,1536]{2,1,0:T(8,128)(2,1)S(1)}, bf16[4,32,1536]{2,1,0:T(8,128)(2,1)S(1)}, u32[]{:S(2)}, u32[]{:S(2)}) collective-permute-start(bf16[4,32,1536]{2,1,0:T(8,128)(2,1)S(1)} %dynamic-slice_bitcast_fusion.13), channel_id=1, source_target_pairs={{0,16},{8,24},{16,0},{24,8},{1,17},{9,25},{17,1},{25,9},{2,18},{10... | collective-permute-start | bytes 1179656 | tf_op jit(solution)/shard_map/ppermute | solution.py:171
  508.8 19.2 %collective-permute-start.50 = (bf16[2,32,2048]{2,1,0:T(8,128)(2,1)S(1)}, bf16[2,32,2048]{2,1,0:T(8,128)(2,1)S(1)}, u32[]{:S(2)}, u32[]{:S(2)}) collective-permute-start(bf16[2,32,2048]{2,1,0:T(8,128)(2,1)S(1)} %dynamic-slice_bitcast_fusion.16), channel_id=1, source_target_pairs={{0,2},{1,3},{2,0},{3,1},{4,6},{5,7},{6,4},{7,5},{8,10},{9,11},{10,... | collective-permute-start | bytes 786440 | tf_op jit(solution)/shard_map/ppermute | solution.py:171
  509.0 24.1 %collective-permute-start.43 = (bf16[2,32,2048]{2,1,0:T(8,128)(2,1)S(1)}, bf16[2,32,2048]{2,1,0:T(8,128)(2,1)S(1)}, u32[]{:S(2)}, u32[]{:S(2)}) collective-permute-start(bf16[2,32,2048]{2,1,0:T(8,128)(2,1)S(1)} %dynamic-slice_bitcast_fusion.17), channel_id=1, source_target_pairs={{0,2},{1,3},{2,0},{3,1},{4,6},{5,7},{6,4},{7,5},{8,10},{9,11},{10,... | collective-permute-start | bytes 786440 | tf_op jit(solution)/shard_map/ppermute | solution.py:171
  512.1 34.9 %collective-permute-start.18 = (bf16[2,32,1536]{2,1,0:T(8,128)(2,1)S(1)}, bf16[2,32,1536]{2,1,0:T(8,128)(2,1)S(1)}, u32[]{:S(2)}, u32[]{:S(2)}) collective-permute-start(bf16[2,32,1536]{2,1,0:T(8,128)(2,1)S(1)} %dynamic-slice_bitcast_fusion.20), channel_id=1, source_target_pairs={{0,2},{1,3},{2,0},{3,1},{4,6},{5,7},{6,4},{7,5},{8,10},{9,11},{10,... | collective-permute-start | bytes 589832 | tf_op jit(solution)/shard_map/ppermute | solution.py:171
  512.4 36.5 %collective-permute-start.11 = (bf16[2,32,1536]{2,1,0:T(8,128)(2,1)S(1)}, bf16[2,32,1536]{2,1,0:T(8,128)(2,1)S(1)}, u32[]{:S(2)}, u32[]{:S(2)}) collective-permute-start(bf16[2,32,1536]{2,1,0:T(8,128)(2,1)S(1)} %dynamic-slice_bitcast_fusion.21), channel_id=1, source_target_pairs={{0,2},{1,3},{2,0},{3,1},{4,6},{5,7},{6,4},{7,5},{8,10},{9,11},{10,... | collective-permute-start | bytes 589832 | tf_op jit(solution)/shard_map/ppermute | solution.py:171
  515.4 53.5 %collective-permute-start.70 = (bf16[4,128,512]{2,1,0:T(8,128)(2,1)S(1)}, bf16[4,128,512]{2,1,0:T(8,128)(2,1)S(1)}, u32[]{:S(2)}, u32[]{:S(2)}) collective-permute-start(bf16[4,128,512]{2,1,0:T(8,128)(2,1)S(1)} %bitcast.583), channel_id=1, source_target_pairs={{0,4},{4,0},{1,5},{5,1},{2,6},{6,2},{3,7},{7,3},{8,12},{12,8},{9,1... | collective-permute-start | bytes 1572872 | tf_op jit(solution)/shard_map/ppermute | solution.py:171
  528.0 41.7 %collective-permute-start.63 = (bf16[4,128,512]{2,1,0:T(8,128)(2,1)S(1)}, bf16[4,128,512]{2,1,0:T(8,128)(2,1)S(1)}, u32[]{:S(2)}, u32[]{:S(2)}) collective-permute-start(bf16[4,128,512]{2,1,0:T(8,128)(2,1)S(1)} %bitcast.584), channel_id=1, source_target_pairs={{0,4},{4,0},{1,5},{5,1},{2,6},{6,2},{3,7},{7,3},{8,12},{12,8},{9,1... | collective-permute-start | bytes 1572872 | tf_op jit(solution)/shard_map/ppermute | solution.py:171
  552.1 15.9 %collective-permute-start.53 = (bf16[2,32,2048]{2,1,0:T(8,128)(2,1)S(1)}, bf16[2,32,2048]{2,1,0:T(8,128)(2,1)S(1)}, u32[]{:S(2)}, u32[]{:S(2)}) collective-permute-start(bf16[2,32,2048]{2,1,0:T(8,128)(2,1)S(1)} %pad_maximum_fusion.31), channel_id=1, source_target_pairs={{0,8},{8,0},{16,24},{24,16},{1,9},{9,1},{17,25},{25,17},{2,10},{10... | collective-permute-start | bytes 786440 | tf_op jit(solution)/shard_map/ppermute | solution.py:171
  (93 other events, 1127.5 us)
Sparse Core Ops, SparseCore 0:
  11.6 80.1 all-gather.2
  95.2 121.0 all-gather.4
